TPU v7x, 32 devices: a whole 2x2x4 slice. The times are simulated.
32 devices in a mesh: gx: 8 (over z, x), gy: 4 (over y, core).
Axes of the slice: x: 2, y: 2, z: 4, core: 2. Of those that a mesh axis runs over, the one named last changes fastest.
Arguments:
- surface: float32 [256, 512], P('gx', 'gy'), may hold values from -6 to 6
- velocity_x: float32 [256, 512], P('gx', 'gy'), may hold values from -3 to 3
- velocity_y: float32 [256, 512], P('gx', 'gy'), may hold values from -3 to 3
- classes: int32 [256, 512], P('gx', 'gy'), may hold values from 0 to 7
- wet_mask: int32 [256, 512], P('gx', 'gy'), may hold values 0 or 1
Outputs:
- surface_final: float32 [256, 512], P('gx', 'gy')
- velocity_x_final: float32 [256, 512], P('gx', 'gy')
- velocity_y_final: float32 [256, 512], P('gx', 'gy')
All inputs are finite; a program needn't handle non-finite values. No bound on the sum of `wet_mask` on one device may be relied on, other than what follows from the above.
Results may differ from a plain program's by a relative error of at most 0.00002.
Values sent between devices are 32-bit elements; how exact they have to be, the bound alone decides.
No kernel may reach another device: no remote copies, remote signals or barrier semaphores. Data moves between devices by JAX's collectives and lax.ppermute only.
A program may use at most 64 MiB of HBM per device.

v0:
```python
import jax
import jax.numpy as jnp
from jax import lax
from jax.sharding import PartitionSpec as P

STEPS = 8


GRAVITY = 1.0
FRICTION = 0.05
TIME_STEP = 1.2


def padded_2(cells, sides, width):
    for axis, dim in sides:
        count = lax.axis_size(axis)
        head = lax.slice_in_dim(cells, 0, width, axis=dim)
        tail = lax.slice_in_dim(cells, cells.shape[dim] - width, cells.shape[dim], axis=dim)
        cells = jnp.concatenate(
            [
                lax.ppermute(tail, axis, [(i, (i + 1) % count) for i in range(count)]),
                cells,
                lax.ppermute(head, axis, [((i + 1) % count, i) for i in range(count)]),
            ],
            axis=dim,
        )
    return cells


def trim_edge(field, width_cut):
    return field[..., width_cut:-width_cut, width_cut:-width_cut]


def diff_first(field):
    return (field[2:, 1:-1] - field[:-2, 1:-1]) * 0.5


def diff_second(field):
    return (field[1:-1, 2:] - field[1:-1, :-2]) * 0.5


def laplacian(field):
    return (
        field[2:, 1:-1]
        + field[:-2, 1:-1]
        + field[1:-1, 2:]
        + field[1:-1, :-2]
        - 4.0 * field[1:-1, 1:-1]
    )


def tendency(state, ground_depth):
    elevation = state[0]
    flow_x = state[1]
    flow_y = state[2]
    wet = (ground_depth > 0.0).astype(jnp.float32)
    change_e = -(diff_first(ground_depth * flow_x) + diff_second(ground_depth * flow_y))
    curved = laplacian(elevation)
    inner = trim_edge(ground_depth, 2)
    coeff = GRAVITY * inner * inner / 3.0
    wet_inner = trim_edge(wet, 2)
    change_x = wet_inner * (
        -GRAVITY * trim_edge(diff_first(elevation), 1)
        - coeff * diff_first(curved)
        - FRICTION * trim_edge(flow_x, 2)
    )
    change_y = wet_inner * (
        -GRAVITY * trim_edge(diff_second(elevation), 1)
        - coeff * diff_second(curved)
        - FRICTION * trim_edge(flow_y, 2)
    )
    return jnp.stack([trim_edge(change_e, 1), change_x, change_y])


def on_device(surface, velocity_x, velocity_y, classes, wet_mask):
    wet = wet_mask.astype(jnp.float32)
    ground_depth = (0.15 + classes.astype(jnp.float32) * (0.4 / 7.0)) * wet
    state = jnp.stack([surface, velocity_x, velocity_y])
    margin = 2
    wide_depth = padded_2(ground_depth, (("gx", 0), ("gy", 1)), margin)

    def section_slope(current):
        padded = padded_2(current, (("gx", 1), ("gy", 2)), 2)
        return tendency(padded, wide_depth)

    for step_index in range(STEPS):
        first = section_slope(state)
        second = section_slope(state + 0.5 * TIME_STEP * first)
        third = section_slope(state + 0.5 * TIME_STEP * second)
        fourth = section_slope(state + TIME_STEP * third)
        state = state + TIME_STEP / 6.0 * (first + 2.0 * second + 2.0 * third + fourth)
    return (state[0], state[1], state[2])


def solution(mesh):
    return jax.shard_map(
        on_device,
        mesh=mesh,
        in_specs=(P("gx", "gy"), P("gx", "gy"), P("gx", "gy"), P("gx", "gy"), P("gx", "gy")),
        out_specs=(P("gx", "gy"), P("gx", "gy"), P("gx", "gy")),
        check_vma=False,
    )
```

profile of v0, /device:TPU:0, one launch (start us, length us, event | category | flops | bytes accessed | tf_op | source)
XLA Modules:
  0.0 361.2 jit_solution(17721447193081352140)
XLA Ops:
  1.4 3.0 collective-permute-start
  4.4 3.1 collective-permute-start.1
  7.6 4.7 %collective-permute-start.5 = (f32[3,2,128]{2,1,0:T(2,128)S(1)}, f32[3,2,128]{2,1,0:T(2,128)S(1)}, u32[]{:S(2)}, u32[]{:S(2)}) collective-permute-start(f32[3,2,128]{2,1,0:T(2,128)S(1)} %get-tuple-element.357), channel_id=1, source_target_pairs={{4,0},{8,4},{12,8},{16,12},{20,16},{24,20},{28,24},{0,28},{5,1},{9... | collective-permute-start | bytes 9224 | tf_op jit(solution)/shard_map/ppermute | solution.py:23
  19.9 4.8 %collective-permute-start.9 = (f32[3,2,128]{2,1,0:T(2,128)S(1)}, f32[3,2,128]{2,1,0:T(2,128)S(1)}, u32[]{:S(2)}, u32[]{:S(2)}) collective-permute-start(f32[3,2,128]{2,1,0:T(2,128)S(1)} %get-tuple-element.355), channel_id=1, source_target_pairs={{4,0},{8,4},{12,8},{16,12},{20,16},{24,20},{28,24},{0,28},{5,1},{9... | collective-permute-start | bytes 9224 | tf_op jit(solution)/shard_map/ppermute | solution.py:23
  28.0 1.9 collective-permute-done.10
  30.7 4.8 %collective-permute-start.13 = (f32[3,2,128]{2,1,0:T(2,128)S(1)}, f32[3,2,128]{2,1,0:T(2,128)S(1)}, u32[]{:S(2)}, u32[]{:S(2)}) collective-permute-start(f32[3,2,128]{2,1,0:T(2,128)S(1)} %get-tuple-element.353), channel_id=1, source_target_pairs={{4,0},{8,4},{12,8},{16,12},{20,16},{24,20},{28,24},{0,28},{5,1},{9... | collective-permute-start | bytes 9224 | tf_op jit(solution)/shard_map/ppermute | solution.py:23
  38.9 1.9 collective-permute-done.14
  41.6 4.8 %collective-permute-start.17 = (f32[3,2,128]{2,1,0:T(2,128)S(1)}, f32[3,2,128]{2,1,0:T(2,128)S(1)}, u32[]{:S(2)}, u32[]{:S(2)}) collective-permute-start(f32[3,2,128]{2,1,0:T(2,128)S(1)} %get-tuple-element.351), channel_id=1, source_target_pairs={{4,0},{8,4},{12,8},{16,12},{20,16},{24,20},{28,24},{0,28},{5,1},{9... | collective-permute-start | bytes 9224 | tf_op jit(solution)/shard_map/ppermute | solution.py:23
  49.8 1.9 collective-permute-done.18
  52.5 4.8 %collective-permute-start.21 = (f32[3,2,128]{2,1,0:T(2,128)S(1)}, f32[3,2,128]{2,1,0:T(2,128)S(1)}, u32[]{:S(2)}, u32[]{:S(2)}) collective-permute-start(f32[3,2,128]{2,1,0:T(2,128)S(1)} %get-tuple-element.349), channel_id=1, source_target_pairs={{4,0},{8,4},{12,8},{16,12},{20,16},{24,20},{28,24},{0,28},{5,1},{9... | collective-permute-start | bytes 9224 | tf_op jit(solution)/shard_map/ppermute | solution.py:23
  60.7 1.9 collective-permute-done.22
  63.4 4.8 %collective-permute-start.25 = (f32[3,2,128]{2,1,0:T(2,128)S(1)}, f32[3,2,128]{2,1,0:T(2,128)S(1)}, u32[]{:S(2)}, u32[]{:S(2)}) collective-permute-start(f32[3,2,128]{2,1,0:T(2,128)S(1)} %get-tuple-element.347), channel_id=1, source_target_pairs={{4,0},{8,4},{12,8},{16,12},{20,16},{24,20},{28,24},{0,28},{5,1},{9... | collective-permute-start | bytes 9224 | tf_op jit(solution)/shard_map/ppermute | solution.py:23
  71.6 1.9 collective-permute-done.26
  74.3 4.8 %collective-permute-start.29 = (f32[3,2,128]{2,1,0:T(2,128)S(1)}, f32[3,2,128]{2,1,0:T(2,128)S(1)}, u32[]{:S(2)}, u32[]{:S(2)}) collective-permute-start(f32[3,2,128]{2,1,0:T(2,128)S(1)} %get-tuple-element.345), channel_id=1, source_target_pairs={{4,0},{8,4},{12,8},{16,12},{20,16},{24,20},{28,24},{0,28},{5,1},{9... | collective-permute-start | bytes 9224 | tf_op jit(solution)/shard_map/ppermute | solution.py:23
  82.5 1.9 collective-permute-done.30
  85.2 4.8 %collective-permute-start.33 = (f32[3,2,128]{2,1,0:T(2,128)S(1)}, f32[3,2,128]{2,1,0:T(2,128)S(1)}, u32[]{:S(2)}, u32[]{:S(2)}) collective-permute-start(f32[3,2,128]{2,1,0:T(2,128)S(1)} %get-tuple-element.343), channel_id=1, source_target_pairs={{4,0},{8,4},{12,8},{16,12},{20,16},{24,20},{28,24},{0,28},{5,1},{9... | collective-permute-start | bytes 9224 | tf_op jit(solution)/shard_map/ppermute | solution.py:23
  93.4 1.9 collective-permute-done.34
  96.1 4.8 %collective-permute-start.37 = (f32[3,2,128]{2,1,0:T(2,128)S(1)}, f32[3,2,128]{2,1,0:T(2,128)S(1)}, u32[]{:S(2)}, u32[]{:S(2)}) collective-permute-start(f32[3,2,128]{2,1,0:T(2,128)S(1)} %get-tuple-element.341), channel_id=1, source_target_pairs={{4,0},{8,4},{12,8},{16,12},{20,16},{24,20},{28,24},{0,28},{5,1},{9... | collective-permute-start | bytes 9224 | tf_op jit(solution)/shard_map/ppermute | solution.py:23
  104.4 1.9 collective-permute-done.38
  107.1 4.8 %collective-permute-start.41 = (f32[3,2,128]{2,1,0:T(2,128)S(1)}, f32[3,2,128]{2,1,0:T(2,128)S(1)}, u32[]{:S(2)}, u32[]{:S(2)}) collective-permute-start(f32[3,2,128]{2,1,0:T(2,128)S(1)} %get-tuple-element.339), channel_id=1, source_target_pairs={{4,0},{8,4},{12,8},{16,12},{20,16},{24,20},{28,24},{0,28},{5,1},{9... | collective-permute-start | bytes 9224 | tf_op jit(solution)/shard_map/ppermute | solution.py:23
  115.3 1.9 collective-permute-done.42
  118.0 4.8 %collective-permute-start.45 = (f32[3,2,128]{2,1,0:T(2,128)S(1)}, f32[3,2,128]{2,1,0:T(2,128)S(1)}, u32[]{:S(2)}, u32[]{:S(2)}) collective-permute-start(f32[3,2,128]{2,1,0:T(2,128)S(1)} %get-tuple-element.337), channel_id=1, source_target_pairs={{4,0},{8,4},{12,8},{16,12},{20,16},{24,20},{28,24},{0,28},{5,1},{9... | collective-permute-start | bytes 9224 | tf_op jit(solution)/shard_map/ppermute | solution.py:23
  126.2 1.9 collective-permute-done.46
  128.9 4.8 %collective-permute-start.49 = (f32[3,2,128]{2,1,0:T(2,128)S(1)}, f32[3,2,128]{2,1,0:T(2,128)S(1)}, u32[]{:S(2)}, u32[]{:S(2)}) collective-permute-start(f32[3,2,128]{2,1,0:T(2,128)S(1)} %get-tuple-element.335), channel_id=1, source_target_pairs={{4,0},{8,4},{12,8},{16,12},{20,16},{24,20},{28,24},{0,28},{5,1},{9... | collective-permute-start | bytes 9224 | tf_op jit(solution)/shard_map/ppermute | solution.py:23
  137.2 1.9 collective-permute-done.50
  139.9 4.8 %collective-permute-start.53 = (f32[3,2,128]{2,1,0:T(2,128)S(1)}, f32[3,2,128]{2,1,0:T(2,128)S(1)}, u32[]{:S(2)}, u32[]{:S(2)}) collective-permute-start(f32[3,2,128]{2,1,0:T(2,128)S(1)} %get-tuple-element.333), channel_id=1, source_target_pairs={{4,0},{8,4},{12,8},{16,12},{20,16},{24,20},{28,24},{0,28},{5,1},{9... | collective-permute-start | bytes 9224 | tf_op jit(solution)/shard_map/ppermute | solution.py:23
  150.9 4.8 %collective-permute-start.57 = (f32[3,2,128]{2,1,0:T(2,128)S(1)}, f32[3,2,128]{2,1,0:T(2,128)S(1)}, u32[]{:S(2)}, u32[]{:S(2)}) collective-permute-start(f32[3,2,128]{2,1,0:T(2,128)S(1)} %get-tuple-element.331), channel_id=1, source_target_pairs={{4,0},{8,4},{12,8},{16,12},{20,16},{24,20},{28,24},{0,28},{5,1},{9... | collective-permute-start | bytes 9224 | tf_op jit(solution)/shard_map/ppermute | solution.py:23
  159.1 1.9 collective-permute-done.58
  161.8 4.8 %collective-permute-start.61 = (f32[3,2,128]{2,1,0:T(2,128)S(1)}, f32[3,2,128]{2,1,0:T(2,128)S(1)}, u32[]{:S(2)}, u32[]{:S(2)}) collective-permute-start(f32[3,2,128]{2,1,0:T(2,128)S(1)} %get-tuple-element.329), channel_id=1, source_target_pairs={{4,0},{8,4},{12,8},{16,12},{20,16},{24,20},{28,24},{0,28},{5,1},{9... | collective-permute-start | bytes 9224 | tf_op jit(solution)/shard_map/ppermute | solution.py:23
  170.1 1.9 collective-permute-done.62
  172.8 4.8 %collective-permute-start.65 = (f32[3,2,128]{2,1,0:T(2,128)S(1)}, f32[3,2,128]{2,1,0:T(2,128)S(1)}, u32[]{:S(2)}, u32[]{:S(2)}) collective-permute-start(f32[3,2,128]{2,1,0:T(2,128)S(1)} %get-tuple-element.327), channel_id=1, source_target_pairs={{4,0},{8,4},{12,8},{16,12},{20,16},{24,20},{28,24},{0,28},{5,1},{9... | collective-permute-start | bytes 9224 | tf_op jit(solution)/shard_map/ppermute | solution.py:23
  181.0 1.9 collective-permute-done.66
  183.8 4.8 %collective-permute-start.69 = (f32[3,2,128]{2,1,0:T(2,128)S(1)}, f32[3,2,128]{2,1,0:T(2,128)S(1)}, u32[]{:S(2)}, u32[]{:S(2)}) collective-permute-start(f32[3,2,128]{2,1,0:T(2,128)S(1)} %get-tuple-element.325), channel_id=1, source_target_pairs={{4,0},{8,4},{12,8},{16,12},{20,16},{24,20},{28,24},{0,28},{5,1},{9... | collective-permute-start | bytes 9224 | tf_op jit(solution)/shard_map/ppermute | solution.py:23
  194.8 4.8 %collective-permute-start.73 = (f32[3,2,128]{2,1,0:T(2,128)S(1)}, f32[3,2,128]{2,1,0:T(2,128)S(1)}, u32[]{:S(2)}, u32[]{:S(2)}) collective-permute-start(f32[3,2,128]{2,1,0:T(2,128)S(1)} %get-tuple-element.323), channel_id=1, source_target_pairs={{4,0},{8,4},{12,8},{16,12},{20,16},{24,20},{28,24},{0,28},{5,1},{9... | collective-permute-start | bytes 9224 | tf_op jit(solution)/shard_map/ppermute | solution.py:23
  205.8 4.8 %collective-permute-start.77 = (f32[3,2,128]{2,1,0:T(2,128)S(1)}, f32[3,2,128]{2,1,0:T(2,128)S(1)}, u32[]{:S(2)}, u32[]{:S(2)}) collective-permute-start(f32[3,2,128]{2,1,0:T(2,128)S(1)} %get-tuple-element.321), channel_id=1, source_target_pairs={{4,0},{8,4},{12,8},{16,12},{20,16},{24,20},{28,24},{0,28},{5,1},{9... | collective-permute-start | bytes 9224 | tf_op jit(solution)/shard_map/ppermute | solution.py:23
  216.8 4.8 %collective-permute-start.81 = (f32[3,2,128]{2,1,0:T(2,128)S(1)}, f32[3,2,128]{2,1,0:T(2,128)S(1)}, u32[]{:S(2)}, u32[]{:S(2)}) collective-permute-start(f32[3,2,128]{2,1,0:T(2,128)S(1)} %get-tuple-element.319), channel_id=1, source_target_pairs={{4,0},{8,4},{12,8},{16,12},{20,16},{24,20},{28,24},{0,28},{5,1},{9... | collective-permute-start | bytes 9224 | tf_op jit(solution)/shard_map/ppermute | solution.py:23
  227.8 4.8 %collective-permute-start.85 = (f32[3,2,128]{2,1,0:T(2,128)S(1)}, f32[3,2,128]{2,1,0:T(2,128)S(1)}, u32[]{:S(2)}, u32[]{:S(2)}) collective-permute-start(f32[3,2,128]{2,1,0:T(2,128)S(1)} %get-tuple-element.317), channel_id=1, source_target_pairs={{4,0},{8,4},{12,8},{16,12},{20,16},{24,20},{28,24},{0,28},{5,1},{9... | collective-permute-start | bytes 9224 | tf_op jit(solution)/shard_map/ppermute | solution.py:23
  238.8 4.8 %collective-permute-start.89 = (f32[3,2,128]{2,1,0:T(2,128)S(1)}, f32[3,2,128]{2,1,0:T(2,128)S(1)}, u32[]{:S(2)}, u32[]{:S(2)}) collective-permute-start(f32[3,2,128]{2,1,0:T(2,128)S(1)} %get-tuple-element.315), channel_id=1, source_target_pairs={{4,0},{8,4},{12,8},{16,12},{20,16},{24,20},{28,24},{0,28},{5,1},{9... | collective-permute-start | bytes 9224 | tf_op jit(solution)/shard_map/ppermute | solution.py:23
  249.9 4.8 %collective-permute-start.93 = (f32[3,2,128]{2,1,0:T(2,128)S(1)}, f32[3,2,128]{2,1,0:T(2,128)S(1)}, u32[]{:S(2)}, u32[]{:S(2)}) collective-permute-start(f32[3,2,128]{2,1,0:T(2,128)S(1)} %get-tuple-element.313), channel_id=1, source_target_pairs={{4,0},{8,4},{12,8},{16,12},{20,16},{24,20},{28,24},{0,28},{5,1},{9... | collective-permute-start | bytes 9224 | tf_op jit(solution)/shard_map/ppermute | solution.py:23
  260.9 4.8 %collective-permute-start.97 = (f32[3,2,128]{2,1,0:T(2,128)S(1)}, f32[3,2,128]{2,1,0:T(2,128)S(1)}, u32[]{:S(2)}, u32[]{:S(2)}) collective-permute-start(f32[3,2,128]{2,1,0:T(2,128)S(1)} %get-tuple-element.311), channel_id=1, source_target_pairs={{4,0},{8,4},{12,8},{16,12},{20,16},{24,20},{28,24},{0,28},{5,1},{9... | collective-permute-start | bytes 9224 | tf_op jit(solution)/shard_map/ppermute | solution.py:23
  272.0 4.8 %collective-permute-start.101 = (f32[3,2,128]{2,1,0:T(2,128)S(1)}, f32[3,2,128]{2,1,0:T(2,128)S(1)}, u32[]{:S(2)}, u32[]{:S(2)}) collective-permute-start(f32[3,2,128]{2,1,0:T(2,128)S(1)} %get-tuple-element.309), channel_id=1, source_target_pairs={{4,0},{8,4},{12,8},{16,12},{20,16},{24,20},{28,24},{0,28},{5,1},{9... | collective-permute-start | bytes 9224 | tf_op jit(solution)/shard_map/ppermute | solution.py:23
  283.0 4.8 %collective-permute-start.105 = (f32[3,2,128]{2,1,0:T(2,128)S(1)}, f32[3,2,128]{2,1,0:T(2,128)S(1)}, u32[]{:S(2)}, u32[]{:S(2)}) collective-permute-start(f32[3,2,128]{2,1,0:T(2,128)S(1)} %get-tuple-element.307), channel_id=1, source_target_pairs={{4,0},{8,4},{12,8},{16,12},{20,16},{24,20},{28,24},{0,28},{5,1},{9... | collective-permute-start | bytes 9224 | tf_op jit(solution)/shard_map/ppermute | solution.py:23
  294.1 4.8 %collective-permute-start.109 = (f32[3,2,128]{2,1,0:T(2,128)S(1)}, f32[3,2,128]{2,1,0:T(2,128)S(1)}, u32[]{:S(2)}, u32[]{:S(2)}) collective-permute-start(f32[3,2,128]{2,1,0:T(2,128)S(1)} %get-tuple-element.305), channel_id=1, source_target_pairs={{4,0},{8,4},{12,8},{16,12},{20,16},{24,20},{28,24},{0,28},{5,1},{9... | collective-permute-start | bytes 9224 | tf_op jit(solution)/shard_map/ppermute | solution.py:23
  305.1 4.8 %collective-permute-start.113 = (f32[3,2,128]{2,1,0:T(2,128)S(1)}, f32[3,2,128]{2,1,0:T(2,128)S(1)}, u32[]{:S(2)}, u32[]{:S(2)}) collective-permute-start(f32[3,2,128]{2,1,0:T(2,128)S(1)} %get-tuple-element.303), channel_id=1, source_target_pairs={{4,0},{8,4},{12,8},{16,12},{20,16},{24,20},{28,24},{0,28},{5,1},{9... | collective-permute-start | bytes 9224 | tf_op jit(solution)/shard_map/ppermute | solution.py:23
  316.2 4.8 %collective-permute-start.117 = (f32[3,2,128]{2,1,0:T(2,128)S(1)}, f32[3,2,128]{2,1,0:T(2,128)S(1)}, u32[]{:S(2)}, u32[]{:S(2)}) collective-permute-start(f32[3,2,128]{2,1,0:T(2,128)S(1)} %get-tuple-element.301), channel_id=1, source_target_pairs={{4,0},{8,4},{12,8},{16,12},{20,16},{24,20},{28,24},{0,28},{5,1},{9... | collective-permute-start | bytes 9224 | tf_op jit(solution)/shard_map/ppermute | solution.py:23
  327.3 4.8 %collective-permute-start.121 = (f32[3,2,128]{2,1,0:T(2,128)S(1)}, f32[3,2,128]{2,1,0:T(2,128)S(1)}, u32[]{:S(2)}, u32[]{:S(2)}) collective-permute-start(f32[3,2,128]{2,1,0:T(2,128)S(1)} %get-tuple-element.299), channel_id=1, source_target_pairs={{4,0},{8,4},{12,8},{16,12},{20,16},{24,20},{28,24},{0,28},{5,1},{9... | collective-permute-start | bytes 9224 | tf_op jit(solution)/shard_map/ppermute | solution.py:23
  338.4 4.8 %collective-permute-start.125 = (f32[3,2,128]{2,1,0:T(2,128)S(1)}, f32[3,2,128]{2,1,0:T(2,128)S(1)}, u32[]{:S(2)}, u32[]{:S(2)}) collective-permute-start(f32[3,2,128]{2,1,0:T(2,128)S(1)} %get-tuple-element.297), channel_id=1, source_target_pairs={{4,0},{8,4},{12,8},{16,12},{20,16},{24,20},{28,24},{0,28},{5,1},{9... | collective-permute-start | bytes 9224 | tf_op jit(solution)/shard_map/ppermute | solution.py:23
  349.5 4.8 %collective-permute-start.129 = (f32[3,2,128]{2,1,0:T(2,128)S(1)}, f32[3,2,128]{2,1,0:T(2,128)S(1)}, u32[]{:S(2)}, u32[]{:S(2)}) collective-permute-start(f32[3,2,128]{2,1,0:T(2,128)S(1)} %get-tuple-element.295), channel_id=1, source_target_pairs={{4,0},{8,4},{12,8},{16,12},{20,16},{24,20},{28,24},{0,28},{5,1},{9... | collective-permute-start | bytes 9224 | tf_op jit(solution)/shard_map/ppermute | solution.py:23
  (613 shorter events, 170.8 us)
Async XLA Ops:
  1.4 10.9 %collective-permute-start = (f32[2,128]{1,0:T(2,128)S(1)}, f32[2,128]{1,0:T(2,128)S(1)}, u32[]{:S(2)}, u32[]{:S(2)}) collective-permute-start(f32[2,128]{1,0:T(2,128)S(1)} %get-tuple-element.648), channel_id=1, source_target_pairs={{0,4},{4,8},{8,12},{12,16},{16,20},{20,24},{24,28},{28,0},{1,5},{5... | collective-permute-start | bytes 3080 | tf_op jit(solution)/shard_map/ppermute | solution.py:21
  4.4 7.9 %collective-permute-start.1 = (f32[2,128]{1,0:T(2,128)S(1)}, f32[2,128]{1,0:T(2,128)S(1)}, u32[]{:S(2)}, u32[]{:S(2)}) collective-permute-start(f32[2,128]{1,0:T(2,128)S(1)} %get-tuple-element.649), channel_id=1, source_target_pairs={{4,0},{8,4},{12,8},{16,12},{20,16},{24,20},{28,24},{0,28},{5,1},{9... | collective-permute-start | bytes 3080 | tf_op jit(solution)/shard_map/ppermute | solution.py:23
  7.6 6.3 %collective-permute-start.4 = (f32[3,2,128]{2,1,0:T(2,128)S(1)}, f32[3,2,128]{2,1,0:T(2,128)S(1)}, u32[]{:S(2)}, u32[]{:S(2)}) collective-permute-start(f32[3,2,128]{2,1,0:T(2,128)S(1)} %get-tuple-element.356), channel_id=1, source_target_pairs={{0,4},{4,8},{8,12},{12,16},{16,20},{20,24},{24,28},{28,0},{1,5},{5... | collective-permute-start | bytes 9224 | tf_op jit(solution)/shard_map/ppermute | solution.py:21
  19.8 6.3 %collective-permute-start.8 = (f32[3,2,128]{2,1,0:T(2,128)S(1)}, f32[3,2,128]{2,1,0:T(2,128)S(1)}, u32[]{:S(2)}, u32[]{:S(2)}) collective-permute-start(f32[3,2,128]{2,1,0:T(2,128)S(1)} %get-tuple-element.354), channel_id=1, source_target_pairs={{0,4},{4,8},{8,12},{12,16},{16,20},{20,24},{24,28},{28,0},{1,5},{5... | collective-permute-start | bytes 9224 | tf_op jit(solution)/shard_map/ppermute | solution.py:21
  30.7 6.4 %collective-permute-start.12 = (f32[3,2,128]{2,1,0:T(2,128)S(1)}, f32[3,2,128]{2,1,0:T(2,128)S(1)}, u32[]{:S(2)}, u32[]{:S(2)}) collective-permute-start(f32[3,2,128]{2,1,0:T(2,128)S(1)} %get-tuple-element.352), channel_id=1, source_target_pairs={{0,4},{4,8},{8,12},{12,16},{16,20},{20,24},{24,28},{28,0},{1,5},{5... | collective-permute-start | bytes 9224 | tf_op jit(solution)/shard_map/ppermute | solution.py:21
  41.5 6.4 %collective-permute-start.16 = (f32[3,2,128]{2,1,0:T(2,128)S(1)}, f32[3,2,128]{2,1,0:T(2,128)S(1)}, u32[]{:S(2)}, u32[]{:S(2)}) collective-permute-start(f32[3,2,128]{2,1,0:T(2,128)S(1)} %get-tuple-element.350), channel_id=1, source_target_pairs={{0,4},{4,8},{8,12},{12,16},{16,20},{20,24},{24,28},{28,0},{1,5},{5... | collective-permute-start | bytes 9224 | tf_op jit(solution)/shard_map/ppermute | solution.py:21
  41.6 6.3 %collective-permute-start.17 = (f32[3,2,128]{2,1,0:T(2,128)S(1)}, f32[3,2,128]{2,1,0:T(2,128)S(1)}, u32[]{:S(2)}, u32[]{:S(2)}) collective-permute-start(f32[3,2,128]{2,1,0:T(2,128)S(1)} %get-tuple-element.351), channel_id=1, source_target_pairs={{4,0},{8,4},{12,8},{16,12},{20,16},{24,20},{28,24},{0,28},{5,1},{9... | collective-permute-start | bytes 9224 | tf_op jit(solution)/shard_map/ppermute | solution.py:23
  52.4 6.4 %collective-permute-start.20 = (f32[3,2,128]{2,1,0:T(2,128)S(1)}, f32[3,2,128]{2,1,0:T(2,128)S(1)}, u32[]{:S(2)}, u32[]{:S(2)}) collective-permute-start(f32[3,2,128]{2,1,0:T(2,128)S(1)} %get-tuple-element.348), channel_id=1, source_target_pairs={{0,4},{4,8},{8,12},{12,16},{16,20},{20,24},{24,28},{28,0},{1,5},{5... | collective-permute-start | bytes 9224 | tf_op jit(solution)/shard_map/ppermute | solution.py:21
  63.3 6.4 %collective-permute-start.24 = (f32[3,2,128]{2,1,0:T(2,128)S(1)}, f32[3,2,128]{2,1,0:T(2,128)S(1)}, u32[]{:S(2)}, u32[]{:S(2)}) collective-permute-start(f32[3,2,128]{2,1,0:T(2,128)S(1)} %get-tuple-element.346), channel_id=1, source_target_pairs={{0,4},{4,8},{8,12},{12,16},{16,20},{20,24},{24,28},{28,0},{1,5},{5... | collective-permute-start | bytes 9224 | tf_op jit(solution)/shard_map/ppermute | solution.py:21
  63.4 6.3 %collective-permute-start.25 = (f32[3,2,128]{2,1,0:T(2,128)S(1)}, f32[3,2,128]{2,1,0:T(2,128)S(1)}, u32[]{:S(2)}, u32[]{:S(2)}) collective-permute-start(f32[3,2,128]{2,1,0:T(2,128)S(1)} %get-tuple-element.347), channel_id=1, source_target_pairs={{4,0},{8,4},{12,8},{16,12},{20,16},{24,20},{28,24},{0,28},{5,1},{9... | collective-permute-start | bytes 9224 | tf_op jit(solution)/shard_map/ppermute | solution.py:23
  74.2 6.4 %collective-permute-start.28 = (f32[3,2,128]{2,1,0:T(2,128)S(1)}, f32[3,2,128]{2,1,0:T(2,128)S(1)}, u32[]{:S(2)}, u32[]{:S(2)}) collective-permute-start(f32[3,2,128]{2,1,0:T(2,128)S(1)} %get-tuple-element.344), channel_id=1, source_target_pairs={{0,4},{4,8},{8,12},{12,16},{16,20},{20,24},{24,28},{28,0},{1,5},{5... | collective-permute-start | bytes 9224 | tf_op jit(solution)/shard_map/ppermute | solution.py:21
  74.3 6.3 %collective-permute-start.29 = (f32[3,2,128]{2,1,0:T(2,128)S(1)}, f32[3,2,128]{2,1,0:T(2,128)S(1)}, u32[]{:S(2)}, u32[]{:S(2)}) collective-permute-start(f32[3,2,128]{2,1,0:T(2,128)S(1)} %get-tuple-element.345), channel_id=1, source_target_pairs={{4,0},{8,4},{12,8},{16,12},{20,16},{24,20},{28,24},{0,28},{5,1},{9... | collective-permute-start | bytes 9224 | tf_op jit(solution)/shard_map/ppermute | solution.py:23
  85.2 6.4 %collective-permute-start.32 = (f32[3,2,128]{2,1,0:T(2,128)S(1)}, f32[3,2,128]{2,1,0:T(2,128)S(1)}, u32[]{:S(2)}, u32[]{:S(2)}) collective-permute-start(f32[3,2,128]{2,1,0:T(2,128)S(1)} %get-tuple-element.342), channel_id=1, source_target_pairs={{0,4},{4,8},{8,12},{12,16},{16,20},{20,24},{24,28},{28,0},{1,5},{5... | collective-permute-start | bytes 9224 | tf_op jit(solution)/shard_map/ppermute | solution.py:21
  85.2 6.3 %collective-permute-start.33 = (f32[3,2,128]{2,1,0:T(2,128)S(1)}, f32[3,2,128]{2,1,0:T(2,128)S(1)}, u32[]{:S(2)}, u32[]{:S(2)}) collective-permute-start(f32[3,2,128]{2,1,0:T(2,128)S(1)} %get-tuple-element.343), channel_id=1, source_target_pairs={{4,0},{8,4},{12,8},{16,12},{20,16},{24,20},{28,24},{0,28},{5,1},{9... | collective-permute-start | bytes 9224 | tf_op jit(solution)/shard_map/ppermute | solution.py:23
  96.1 6.4 %collective-permute-start.36 = (f32[3,2,128]{2,1,0:T(2,128)S(1)}, f32[3,2,128]{2,1,0:T(2,128)S(1)}, u32[]{:S(2)}, u32[]{:S(2)}) collective-permute-start(f32[3,2,128]{2,1,0:T(2,128)S(1)} %get-tuple-element.340), channel_id=1, source_target_pairs={{0,4},{4,8},{8,12},{12,16},{16,20},{20,24},{24,28},{28,0},{1,5},{5... | collective-permute-start | bytes 9224 | tf_op jit(solution)/shard_map/ppermute | solution.py:21
  96.1 6.3 %collective-permute-start.37 = (f32[3,2,128]{2,1,0:T(2,128)S(1)}, f32[3,2,128]{2,1,0:T(2,128)S(1)}, u32[]{:S(2)}, u32[]{:S(2)}) collective-permute-start(f32[3,2,128]{2,1,0:T(2,128)S(1)} %get-tuple-element.341), channel_id=1, source_target_pairs={{4,0},{8,4},{12,8},{16,12},{20,16},{24,20},{28,24},{0,28},{5,1},{9... | collective-permute-start | bytes 9224 | tf_op jit(solution)/shard_map/ppermute | solution.py:23
  107.0 6.4 %collective-permute-start.40 = (f32[3,2,128]{2,1,0:T(2,128)S(1)}, f32[3,2,128]{2,1,0:T(2,128)S(1)}, u32[]{:S(2)}, u32[]{:S(2)}) collective-permute-start(f32[3,2,128]{2,1,0:T(2,128)S(1)} %get-tuple-element.338), channel_id=1, source_target_pairs={{0,4},{4,8},{8,12},{12,16},{16,20},{20,24},{24,28},{28,0},{1,5},{5... | collective-permute-start | bytes 9224 | tf_op jit(solution)/shard_map/ppermute | solution.py:21
  107.1 6.3 %collective-permute-start.41 = (f32[3,2,128]{2,1,0:T(2,128)S(1)}, f32[3,2,128]{2,1,0:T(2,128)S(1)}, u32[]{:S(2)}, u32[]{:S(2)}) collective-permute-start(f32[3,2,128]{2,1,0:T(2,128)S(1)} %get-tuple-element.339), channel_id=1, source_target_pairs={{4,0},{8,4},{12,8},{16,12},{20,16},{24,20},{28,24},{0,28},{5,1},{9... | collective-permute-start | bytes 9224 | tf_op jit(solution)/shard_map/ppermute | solution.py:23
  117.9 6.4 %collective-permute-start.44 = (f32[3,2,128]{2,1,0:T(2,128)S(1)}, f32[3,2,128]{2,1,0:T(2,128)S(1)}, u32[]{:S(2)}, u32[]{:S(2)}) collective-permute-start(f32[3,2,128]{2,1,0:T(2,128)S(1)} %get-tuple-element.336), channel_id=1, source_target_pairs={{0,4},{4,8},{8,12},{12,16},{16,20},{20,24},{24,28},{28,0},{1,5},{5... | collective-permute-start | bytes 9224 | tf_op jit(solution)/shard_map/ppermute | solution.py:21
  118.0 6.3 %collective-permute-start.45 = (f32[3,2,128]{2,1,0:T(2,128)S(1)}, f32[3,2,128]{2,1,0:T(2,128)S(1)}, u32[]{:S(2)}, u32[]{:S(2)}) collective-permute-start(f32[3,2,128]{2,1,0:T(2,128)S(1)} %get-tuple-element.337), channel_id=1, source_target_pairs={{4,0},{8,4},{12,8},{16,12},{20,16},{24,20},{28,24},{0,28},{5,1},{9... | collective-permute-start | bytes 9224 | tf_op jit(solution)/shard_map/ppermute | solution.py:23
  128.9 6.4 %collective-permute-start.48 = (f32[3,2,128]{2,1,0:T(2,128)S(1)}, f32[3,2,128]{2,1,0:T(2,128)S(1)}, u32[]{:S(2)}, u32[]{:S(2)}) collective-permute-start(f32[3,2,128]{2,1,0:T(2,128)S(1)} %get-tuple-element.334), channel_id=1, source_target_pairs={{0,4},{4,8},{8,12},{12,16},{16,20},{20,24},{24,28},{28,0},{1,5},{5... | collective-permute-start | bytes 9224 | tf_op jit(solution)/shard_map/ppermute | solution.py:21
  128.9 6.3 %collective-permute-start.49 = (f32[3,2,128]{2,1,0:T(2,128)S(1)}, f32[3,2,128]{2,1,0:T(2,128)S(1)}, u32[]{:S(2)}, u32[]{:S(2)}) collective-permute-start(f32[3,2,128]{2,1,0:T(2,128)S(1)} %get-tuple-element.335), channel_id=1, source_target_pairs={{4,0},{8,4},{12,8},{16,12},{20,16},{24,20},{28,24},{0,28},{5,1},{9... | collective-permute-start | bytes 9224 | tf_op jit(solution)/shard_map/ppermute | solution.py:23
  139.8 6.4 %collective-permute-start.52 = (f32[3,2,128]{2,1,0:T(2,128)S(1)}, f32[3,2,128]{2,1,0:T(2,128)S(1)}, u32[]{:S(2)}, u32[]{:S(2)}) collective-permute-start(f32[3,2,128]{2,1,0:T(2,128)S(1)} %get-tuple-element.332), channel_id=1, source_target_pairs={{0,4},{4,8},{8,12},{12,16},{16,20},{20,24},{24,28},{28,0},{1,5},{5... | collective-permute-start | bytes 9224 | tf_op jit(solution)/shard_map/ppermute | solution.py:21
  139.9 6.3 %collective-permute-start.53 = (f32[3,2,128]{2,1,0:T(2,128)S(1)}, f32[3,2,128]{2,1,0:T(2,128)S(1)}, u32[]{:S(2)}, u32[]{:S(2)}) collective-permute-start(f32[3,2,128]{2,1,0:T(2,128)S(1)} %get-tuple-element.333), channel_id=1, source_target_pairs={{4,0},{8,4},{12,8},{16,12},{20,16},{24,20},{28,24},{0,28},{5,1},{9... | collective-permute-start | bytes 9224 | tf_op jit(solution)/shard_map/ppermute | solution.py:23
  150.8 6.4 %collective-permute-start.56 = (f32[3,2,128]{2,1,0:T(2,128)S(1)}, f32[3,2,128]{2,1,0:T(2,128)S(1)}, u32[]{:S(2)}, u32[]{:S(2)}) collective-permute-start(f32[3,2,128]{2,1,0:T(2,128)S(1)} %get-tuple-element.330), channel_id=1, source_target_pairs={{0,4},{4,8},{8,12},{12,16},{16,20},{20,24},{24,28},{28,0},{1,5},{5... | collective-permute-start | bytes 9224 | tf_op jit(solution)/shard_map/ppermute | solution.py:21
  150.9 6.3 %collective-permute-start.57 = (f32[3,2,128]{2,1,0:T(2,128)S(1)}, f32[3,2,128]{2,1,0:T(2,128)S(1)}, u32[]{:S(2)}, u32[]{:S(2)}) collective-permute-start(f32[3,2,128]{2,1,0:T(2,128)S(1)} %get-tuple-element.331), channel_id=1, source_target_pairs={{4,0},{8,4},{12,8},{16,12},{20,16},{24,20},{28,24},{0,28},{5,1},{9... | collective-permute-start | bytes 9224 | tf_op jit(solution)/shard_map/ppermute | solution.py:23
  161.8 6.4 %collective-permute-start.60 = (f32[3,2,128]{2,1,0:T(2,128)S(1)}, f32[3,2,128]{2,1,0:T(2,128)S(1)}, u32[]{:S(2)}, u32[]{:S(2)}) collective-permute-start(f32[3,2,128]{2,1,0:T(2,128)S(1)} %get-tuple-element.328), channel_id=1, source_target_pairs={{0,4},{4,8},{8,12},{12,16},{16,20},{20,24},{24,28},{28,0},{1,5},{5... | collective-permute-start | bytes 9224 | tf_op jit(solution)/shard_map/ppermute | solution.py:21
  161.8 6.3 %collective-permute-start.61 = (f32[3,2,128]{2,1,0:T(2,128)S(1)}, f32[3,2,128]{2,1,0:T(2,128)S(1)}, u32[]{:S(2)}, u32[]{:S(2)}) collective-permute-start(f32[3,2,128]{2,1,0:T(2,128)S(1)} %get-tuple-element.329), channel_id=1, source_target_pairs={{4,0},{8,4},{12,8},{16,12},{20,16},{24,20},{28,24},{0,28},{5,1},{9... | collective-permute-start | bytes 9224 | tf_op jit(solution)/shard_map/ppermute | solution.py:23
  172.7 6.4 %collective-permute-start.64 = (f32[3,2,128]{2,1,0:T(2,128)S(1)}, f32[3,2,128]{2,1,0:T(2,128)S(1)}, u32[]{:S(2)}, u32[]{:S(2)}) collective-permute-start(f32[3,2,128]{2,1,0:T(2,128)S(1)} %get-tuple-element.326), channel_id=1, source_target_pairs={{0,4},{4,8},{8,12},{12,16},{16,20},{20,24},{24,28},{28,0},{1,5},{5... | collective-permute-start | bytes 9224 | tf_op jit(solution)/shard_map/ppermute | solution.py:21
  183.7 6.4 %collective-permute-start.68 = (f32[3,2,128]{2,1,0:T(2,128)S(1)}, f32[3,2,128]{2,1,0:T(2,128)S(1)}, u32[]{:S(2)}, u32[]{:S(2)}) collective-permute-start(f32[3,2,128]{2,1,0:T(2,128)S(1)} %get-tuple-element.324), channel_id=1, source_target_pairs={{0,4},{4,8},{8,12},{12,16},{16,20},{20,24},{24,28},{28,0},{1,5},{5... | collective-permute-start | bytes 9224 | tf_op jit(solution)/shard_map/ppermute | solution.py:21
  183.8 6.3 %collective-permute-start.69 = (f32[3,2,128]{2,1,0:T(2,128)S(1)}, f32[3,2,128]{2,1,0:T(2,128)S(1)}, u32[]{:S(2)}, u32[]{:S(2)}) collective-permute-start(f32[3,2,128]{2,1,0:T(2,128)S(1)} %get-tuple-element.325), channel_id=1, source_target_pairs={{4,0},{8,4},{12,8},{16,12},{20,16},{24,20},{28,24},{0,28},{5,1},{9... | collective-permute-start | bytes 9224 | tf_op jit(solution)/shard_map/ppermute | solution.py:23
  194.7 6.4 %collective-permute-start.72 = (f32[3,2,128]{2,1,0:T(2,128)S(1)}, f32[3,2,128]{2,1,0:T(2,128)S(1)}, u32[]{:S(2)}, u32[]{:S(2)}) collective-permute-start(f32[3,2,128]{2,1,0:T(2,128)S(1)} %get-tuple-element.322), channel_id=1, source_target_pairs={{0,4},{4,8},{8,12},{12,16},{16,20},{20,24},{24,28},{28,0},{1,5},{5... | collective-permute-start | bytes 9224 | tf_op jit(solution)/shard_map/ppermute | solution.py:21
  194.8 6.3 %collective-permute-start.73 = (f32[3,2,128]{2,1,0:T(2,128)S(1)}, f32[3,2,128]{2,1,0:T(2,128)S(1)}, u32[]{:S(2)}, u32[]{:S(2)}) collective-permute-start(f32[3,2,128]{2,1,0:T(2,128)S(1)} %get-tuple-element.323), channel_id=1, source_target_pairs={{4,0},{8,4},{12,8},{16,12},{20,16},{24,20},{28,24},{0,28},{5,1},{9... | collective-permute-start | bytes 9224 | tf_op jit(solution)/shard_map/ppermute | solution.py:23
  205.7 6.4 %collective-permute-start.76 = (f32[3,2,128]{2,1,0:T(2,128)S(1)}, f32[3,2,128]{2,1,0:T(2,128)S(1)}, u32[]{:S(2)}, u32[]{:S(2)}) collective-permute-start(f32[3,2,128]{2,1,0:T(2,128)S(1)} %get-tuple-element.320), channel_id=1, source_target_pairs={{0,4},{4,8},{8,12},{12,16},{16,20},{20,24},{24,28},{28,0},{1,5},{5... | collective-permute-start | bytes 9224 | tf_op jit(solution)/shard_map/ppermute | solution.py:21
  205.8 6.3 %collective-permute-start.77 = (f32[3,2,128]{2,1,0:T(2,128)S(1)}, f32[3,2,128]{2,1,0:T(2,128)S(1)}, u32[]{:S(2)}, u32[]{:S(2)}) collective-permute-start(f32[3,2,128]{2,1,0:T(2,128)S(1)} %get-tuple-element.321), channel_id=1, source_target_pairs={{4,0},{8,4},{12,8},{16,12},{20,16},{24,20},{28,24},{0,28},{5,1},{9... | collective-permute-start | bytes 9224 | tf_op jit(solution)/shard_map/ppermute | solution.py:23
  216.7 6.4 %collective-permute-start.80 = (f32[3,2,128]{2,1,0:T(2,128)S(1)}, f32[3,2,128]{2,1,0:T(2,128)S(1)}, u32[]{:S(2)}, u32[]{:S(2)}) collective-permute-start(f32[3,2,128]{2,1,0:T(2,128)S(1)} %get-tuple-element.318), channel_id=1, source_target_pairs={{0,4},{4,8},{8,12},{12,16},{16,20},{20,24},{24,28},{28,0},{1,5},{5... | collective-permute-start | bytes 9224 | tf_op jit(solution)/shard_map/ppermute | solution.py:21
  227.7 6.4 %collective-permute-start.84 = (f32[3,2,128]{2,1,0:T(2,128)S(1)}, f32[3,2,128]{2,1,0:T(2,128)S(1)}, u32[]{:S(2)}, u32[]{:S(2)}) collective-permute-start(f32[3,2,128]{2,1,0:T(2,128)S(1)} %get-tuple-element.316), channel_id=1, source_target_pairs={{0,4},{4,8},{8,12},{12,16},{16,20},{20,24},{24,28},{28,0},{1,5},{5... | collective-permute-start | bytes 9224 | tf_op jit(solution)/shard_map/ppermute | solution.py:21
  238.8 6.4 %collective-permute-start.88 = (f32[3,2,128]{2,1,0:T(2,128)S(1)}, f32[3,2,128]{2,1,0:T(2,128)S(1)}, u32[]{:S(2)}, u32[]{:S(2)}) collective-permute-start(f32[3,2,128]{2,1,0:T(2,128)S(1)} %get-tuple-element.314), channel_id=1, source_target_pairs={{0,4},{4,8},{8,12},{12,16},{16,20},{20,24},{24,28},{28,0},{1,5},{5... | collective-permute-start | bytes 9224 | tf_op jit(solution)/shard_map/ppermute | solution.py:21
  249.8 6.4 %collective-permute-start.92 = (f32[3,2,128]{2,1,0:T(2,128)S(1)}, f32[3,2,128]{2,1,0:T(2,128)S(1)}, u32[]{:S(2)}, u32[]{:S(2)}) collective-permute-start(f32[3,2,128]{2,1,0:T(2,128)S(1)} %get-tuple-element.312), channel_id=1, source_target_pairs={{0,4},{4,8},{8,12},{12,16},{16,20},{20,24},{24,28},{28,0},{1,5},{5... | collective-permute-start | bytes 9224 | tf_op jit(solution)/shard_map/ppermute | solution.py:21
  260.8 6.4 %collective-permute-start.96 = (f32[3,2,128]{2,1,0:T(2,128)S(1)}, f32[3,2,128]{2,1,0:T(2,128)S(1)}, u32[]{:S(2)}, u32[]{:S(2)}) collective-permute-start(f32[3,2,128]{2,1,0:T(2,128)S(1)} %get-tuple-element.310), channel_id=1, source_target_pairs={{0,4},{4,8},{8,12},{12,16},{16,20},{20,24},{24,28},{28,0},{1,5},{5... | collective-permute-start | bytes 9224 | tf_op jit(solution)/shard_map/ppermute | solution.py:21
  271.9 6.4 %collective-permute-start.100 = (f32[3,2,128]{2,1,0:T(2,128)S(1)}, f32[3,2,128]{2,1,0:T(2,128)S(1)}, u32[]{:S(2)}, u32[]{:S(2)}) collective-permute-start(f32[3,2,128]{2,1,0:T(2,128)S(1)} %get-tuple-element.308), channel_id=1, source_target_pairs={{0,4},{4,8},{8,12},{12,16},{16,20},{20,24},{24,28},{28,0},{1,5},{5... | collective-permute-start | bytes 9224 | tf_op jit(solution)/shard_map/ppermute | solution.py:21
  283.0 6.4 %collective-permute-start.104 = (f32[3,2,128]{2,1,0:T(2,128)S(1)}, f32[3,2,128]{2,1,0:T(2,128)S(1)}, u32[]{:S(2)}, u32[]{:S(2)}) collective-permute-start(f32[3,2,128]{2,1,0:T(2,128)S(1)} %get-tuple-element.306), channel_id=1, source_target_pairs={{0,4},{4,8},{8,12},{12,16},{16,20},{20,24},{24,28},{28,0},{1,5},{5... | collective-permute-start | bytes 9224 | tf_op jit(solution)/shard_map/ppermute | solution.py:21
  294.0 6.4 %collective-permute-start.108 = (f32[3,2,128]{2,1,0:T(2,128)S(1)}, f32[3,2,128]{2,1,0:T(2,128)S(1)}, u32[]{:S(2)}, u32[]{:S(2)}) collective-permute-start(f32[3,2,128]{2,1,0:T(2,128)S(1)} %get-tuple-element.304), channel_id=1, source_target_pairs={{0,4},{4,8},{8,12},{12,16},{16,20},{20,24},{24,28},{28,0},{1,5},{5... | collective-permute-start | bytes 9224 | tf_op jit(solution)/shard_map/ppermute | solution.py:21
  305.1 6.4 %collective-permute-start.112 = (f32[3,2,128]{2,1,0:T(2,128)S(1)}, f32[3,2,128]{2,1,0:T(2,128)S(1)}, u32[]{:S(2)}, u32[]{:S(2)}) collective-permute-start(f32[3,2,128]{2,1,0:T(2,128)S(1)} %get-tuple-element.302), channel_id=1, source_target_pairs={{0,4},{4,8},{8,12},{12,16},{16,20},{20,24},{24,28},{28,0},{1,5},{5... | collective-permute-start | bytes 9224 | tf_op jit(solution)/shard_map/ppermute | solution.py:21
  316.2 6.4 %collective-permute-start.116 = (f32[3,2,128]{2,1,0:T(2,128)S(1)}, f32[3,2,128]{2,1,0:T(2,128)S(1)}, u32[]{:S(2)}, u32[]{:S(2)}) collective-permute-start(f32[3,2,128]{2,1,0:T(2,128)S(1)} %get-tuple-element.300), channel_id=1, source_target_pairs={{0,4},{4,8},{8,12},{12,16},{16,20},{20,24},{24,28},{28,0},{1,5},{5... | collective-permute-start | bytes 9224 | tf_op jit(solution)/shard_map/ppermute | solution.py:21
  327.3 6.4 %collective-permute-start.120 = (f32[3,2,128]{2,1,0:T(2,128)S(1)}, f32[3,2,128]{2,1,0:T(2,128)S(1)}, u32[]{:S(2)}, u32[]{:S(2)}) collective-permute-start(f32[3,2,128]{2,1,0:T(2,128)S(1)} %get-tuple-element.298), channel_id=1, source_target_pairs={{0,4},{4,8},{8,12},{12,16},{16,20},{20,24},{24,28},{28,0},{1,5},{5... | collective-permute-start | bytes 9224 | tf_op jit(solution)/shard_map/ppermute | solution.py:21
  338.4 6.4 %collective-permute-start.124 = (f32[3,2,128]{2,1,0:T(2,128)S(1)}, f32[3,2,128]{2,1,0:T(2,128)S(1)}, u32[]{:S(2)}, u32[]{:S(2)}) collective-permute-start(f32[3,2,128]{2,1,0:T(2,128)S(1)} %get-tuple-element.296), channel_id=1, source_target_pairs={{0,4},{4,8},{8,12},{12,16},{16,20},{20,24},{24,28},{28,0},{1,5},{5... | collective-permute-start | bytes 9224 | tf_op jit(solution)/shard_map/ppermute | solution.py:21
  349.4 6.4 %collective-permute-start.128 = (f32[3,2,128]{2,1,0:T(2,128)S(1)}, f32[3,2,128]{2,1,0:T(2,128)S(1)}, u32[]{:S(2)}, u32[]{:S(2)}) collective-permute-start(f32[3,2,128]{2,1,0:T(2,128)S(1)} %get-tuple-element.294), channel_id=1, source_target_pairs={{0,4},{4,8},{8,12},{12,16},{16,20},{20,24},{24,28},{28,0},{1,5},{5... | collective-permute-start | bytes 9224 | tf_op jit(solution)/shard_map/ppermute | solution.py:21
  (87 other events, 350.6 us)
where the time goes:
time: 363 us; the launch traced here: 361 us
  starting transfers between devices  221 us (61%)
  waiting for transfers between devices  109 us (30%)
  other arithmetic  19.3 us (5%)
  local copies, waits for them, and re-layouts  8.95 us (2%)
    ppermute x66, starting transfers between devices, padded_2(): lax.ppermute(head, axis, [((i + 1) % count, i) for i in range(count)])  190 us
    ppermute x66, waiting for transfers between devices, padded_2(): lax.ppermute(tail, axis, [(i, (i + 1) % count) for i in range(count)])  109 us
    ppermute x66, starting transfers between devices, padded_2(): lax.ppermute(tail, axis, [(i, (i + 1) % count) for i in range(count)])  30.6 us
  transfers between devices with their start and end apart: 132, of which 65 were waited for; matrix products, arithmetic and copies ran while one was open for 0% of the time, Pallas kernels for 0%

commit v1 on v0

v1 whole, which is shorter than its diff:
```python
import functools
import math

import jax
import jax.numpy as jnp
from jax import lax
from jax.experimental import pallas as pl
from jax.experimental.pallas import tpu as pltpu
from jax.sharding import PartitionSpec as P

STEPS = 8

GRAVITY = 1.0
FRICTION = 0.05
TIME_STEP = 1.2

HALO = 3 * 2 * STEPS
ROW = 8
FULL = 32
AHEAD = 5
LAG = 8
SEAM = 2
UNROLL = 2
VMEM_LIMIT = 8 * 1024 * 1024

R = FRICTION
POWERS = [
    (1, 0, 0, 0, 0, 0),
    (0, 1, 0, 0, 0, 0),
    (0, -R, 1, 0, 0, 0),
    (0, R**2, -R, 1, 0, 0),
    (0, -(R**3), R**2, -2 * R, 1, 0),
    (0, R**4, -(R**3), 3 * R**2, -2 * R, 1),
]
TAYLOR = [TIME_STEP**n / math.factorial(n) for n in range(5)]
E_NEXT = [sum(TAYLOR[n] * POWERS[n][i] for n in range(5)) for i in range(6)]
G_NEXT = [sum(TAYLOR[n] * POWERS[n + 1][i] for n in range(5)) for i in range(6)]
W_NEXT = [
    sum(TAYLOR[n] * (-R) ** (n - 1 - m) * POWERS[m][i] for n in range(1, 5) for m in range(n))
    for i in range(6)
]
DAMP = sum(TAYLOR[n] * (-R) ** n for n in range(5))

G_SCALE = E_NEXT[1]
K_SCALE = (E_NEXT[2], E_NEXT[4] / E_NEXT[2])
W_SCALE = W_NEXT[0]
KEPT = (1.0, G_SCALE, K_SCALE[0], G_SCALE * K_SCALE[0], K_SCALE[0] * K_SCALE[1], G_SCALE * K_SCALE[0] * K_SCALE[1])
E_MIX = E_NEXT[3] / KEPT[3]
G_MIX = [G_SCALE * weight / kept for weight, kept in zip(G_NEXT, KEPT)]
W_MIX = [weight / (W_SCALE * kept) for weight, kept in zip(W_NEXT, KEPT)]


def move(cells, axis, steps):
    count = lax.axis_size(axis)
    return lax.ppermute(cells, axis, [(i, (i + steps[i % len(steps)]) % count) for i in range(count)])


MOVES = ((2, 2, -1, 1), (-1, 1, 2, 2), (1, -1), (-2,))
OUTER, INNER = (-1, 1), (1, -1)


def is_at(axis, period, *places):
    at = lax.rem(lax.axis_index(axis), period)
    return functools.reduce(jnp.logical_or, [at == place for place in places])


def turned(block, by, axis):
    return pltpu.roll(block, by % block.shape[axis], axis)


def fold(first, second):
    lane = lax.broadcasted_iota(jnp.int32, first.shape, 1)
    return jnp.where(lane < 64, pltpu.roll(first, 96, 1), pltpu.roll(second, 32, 1))


def unfold(both):
    return pltpu.roll(both, 32, 1), pltpu.roll(both, 96, 1)


def gather_kernel(got_4, got_3, got_2, got_1, own, centre, to_outer, to_inner, ends, low, high):
    rest = got_4.shape[1]
    place = [is_at("gx", 4, i) for i in range(4)]
    lower_half = is_at("gx", 4, 0, 1)

    def strip(f):
        one, two, three = got_1[f], got_2[f], got_3[f]
        return jnp.concatenate(
            [
                jnp.where(lower_half, two[-rest:], one[-rest:]),
                jnp.where(place[0], one, jnp.where(place[2], two, three)),
                own[f],
                jnp.where(place[1], one, jnp.where(place[3], two, three)),
                got_4[f],
            ],
            axis=0,
        ).T

    e, p, q, depth = (strip(f) for f in range(4))
    length = q.shape[0]
    row = lax.broadcasted_iota(jnp.int32, q.shape, 0)
    north = jnp.where(row == length - 1, 0.0, turned(q, -1, 0))
    south = jnp.where(row == 0, 0.0, turned(q, 1, 0))
    g = (-0.5 * G_SCALE) * ((turned(p, -1, 1) - turned(p, 1, 1)) + (north - south))
    ends[0:ROW], ends[ROW:] = q[:ROW], q[-ROW:]
    for f, part in enumerate((e, g, depth)):
        centre[f] = part
        at = f * (FULL + ROW)
        low[at:at + FULL] = part[:FULL]
        low[at + FULL:at + FULL + ROW] = fold(part[FULL:FULL + ROW], part[FULL + ROW:HALO])
        high[at:at + ROW] = fold(part[-HALO:ROW - HALO], part[ROW - HALO:-FULL])
        high[at + ROW:at + ROW + FULL] = part[-FULL:]
    at = 3 * (FULL + ROW)
    low[at:], high[at:] = q[:ROW], q[-ROW:]
    first_y = is_at("gy", 2, 0)
    to_inner[...] = jnp.where(first_y, high[...], low[...])
    to_outer[...] = jnp.where(first_y, low[...], high[...])


def weighted(weights, values):
    total = None
    for weight, value in zip(weights, values):
        if weight:
            term = value if weight == 1 else weight * value
            total = term if total is None else total + term
    return total


class Rows:
    def __init__(self, blocks, source):
        self.blocks, self.source = blocks, source

    def __getitem__(self, k):
        return self.source[k]

    def __setitem__(self, k, value):
        self.source[k] = value

    def north(self, k):
        return self[k + 1] if k < self.blocks - 1 else turned(self[0], -1, 0)

    def south(self, k):
        return self[k - 1] if k > 0 else turned(self[self.blocks - 1], 1, 0)


class Slope:
    def __init__(self, blocks, ref, alpha, beta, alpha_east, beta_east, diverge=True):
        self.field = Rows(blocks, ref)
        self.alpha, self.beta, self.alpha_east, self.beta_east = alpha, beta, alpha_east, beta_east
        self.diverge = diverge
        self.east_2, self.along, self.sums_east, self.wait, self.x_west = {}, {}, {}, {}, {}
        self.dy, self.lift = {}, {}
        self.sums, self.y = Rows(blocks, {}), Rows(blocks, {})

    def rotate(self, k):
        self.east_2[k] = turned(self.field[k], -2, 1)

    def rotate_sum(self, k):
        here, east_2 = self.field[k], self.east_2.pop(k)
        self.along[k] = turned(east_2 + here, 1, 1)
        self.wait[k] = self.alpha_east[k] * (east_2 - here)

    def sum_up(self, k):
        north, south = self.field.north(k), self.field.south(k)
        self.dy[k] = north - south
        total = self.along.pop(k) + (north + south)
        self.sums[k] = total
        self.sums_east[k] = turned(total, -2, 1)

    def slope_y(self, k):
        s = self.sums
        self.y[k] = self.alpha[k] * self.dy.pop(k) + self.beta[k] * (s.north(k) - s.south(k))

    def lift_y(self, k):
        if self.diverge:
            self.lift[k] = self.y.north(k) - self.y.south(k)

    def slope_x(self, k):
        x = self.wait.pop(k) + self.beta_east[k] * (self.sums_east.pop(k) - self.sums[k])
        self.x_west[k] = turned(x, 2 if self.diverge else 1, 1)
        if self.diverge:
            self.wait[k] = x + self.lift.pop(k)

    def divergence(self, k):
        return self.wait.pop(k) - self.x_west.pop(k)


class Memo:
    def __init__(self, make):
        self.make, self.made = make, {}

    def __getitem__(self, k):
        if k not in self.made:
            self.made[k] = self.make(k)
        return self.made[k]


def parts_of(blocks):
    top = 2 * AHEAD
    assert top + 2 * LAG <= blocks - 2 and 4 + 2 * SEAM <= LAG
    return (
        ("finish", top + 2 * LAG, 2),
        ("sum_up", top, 0),
        ("slope_y", top + 2, 1),
        ("lift_y", top + 4, 2),
        ("slope_x", top + LAG, 2),
        ("rotate_sum", AHEAD, 0),
        ("rotate", 0, 0),
    )


def emit(blocks, sweeps):
    edge = {
        "slope_y": {0: 1, blocks - 1: 1},
        "lift_y": {0: 2, blocks - 1: 2, 1: 1, blocks - 2: 1},
    }
    parts = parts_of(blocks)
    slots = {}
    for number, (slopes, finish) in enumerate(sweeps):
        for order, (name, begin, ahead) in enumerate(parts):
            for i in range(blocks):
                k = (i + ahead + 3 * number) % blocks
                slot = number * blocks + begin + i + SEAM * edge.get(name, {}).get(k, 0)
                slots.setdefault(slot, []).append((number, order, name, k))
    for slot in sorted(slots):
        for number, _, name, k in sorted(slots[slot]):
            slopes, finish = sweeps[number]
            if name == "finish":
                finish(k)
            else:
                for slope in slopes:
                    getattr(slope, name)(k)


def step_kernel(outer, inner, centre, ends, own, flow_x, flow_y, out_e, out_x, out_y,
                rows, low, high, e, g, e1, g1, total_e, *coefficients):
    length = centre.shape[1]
    total = length + 2 * HALO
    blocks = total // ROW
    first_y = is_at("gy", 2, 0)
    low[...] = jnp.where(first_y, outer[...], inner[...])
    high[...] = jnp.where(first_y, inner[...], outer[...])
    for f in range(3):
        at = f * (FULL + ROW)
        rows[f, 0:ROW], rows[f, ROW:2 * ROW] = unfold(low[at:at + ROW])
        rows[f, 2 * ROW:HALO] = low[at + ROW:at + ROW + FULL]
        rows[f, HALO:HALO + length] = centre[f]
        rows[f, HALO + length:HALO + length + FULL] = high[at:at + FULL]
        rows[f, total - 2 * ROW:total - ROW], rows[f, total - ROW:total] = unfold(high[at + FULL:at + FULL + ROW])
    last = 3 * (FULL + ROW)
    for at, given in (
        (HALO, low[last + ROW - 1:last + ROW]),
        (HALO + length - 1, -high[last:last + 1]),
        (HALO - 1, -ends[0:1]),
        (HALO + length, ends[2 * ROW - 1:2 * ROW]),
    ):
        rows[1, at:at + 1] = rows[1, at:at + 1] + (0.5 * G_SCALE) * given

    def strided(k):
        return pl.ds(k, ROW, stride=blocks)

    for k in range(blocks):
        e[k] = rows[0, strided(k), :]
        g[k] = rows[1, strided(k), :]
        total_e[k] = jnp.zeros((ROW, e.shape[2]), jnp.float32)
        depth = rows[2, strided(k), :]
        cube = depth * depth * depth * (GRAVITY / 12.0)
        slow = 0.25 * GRAVITY * depth - 4.0 * cube
        both = (slow, cube, turned(slow, -1, 1), turned(cube, -1, 1))
        for n in range(2):
            for ref, value in zip(coefficients[4 * n:4 * n + 4], both):
                ref[k] = K_SCALE[n] * value

    def slopes_of(n, *refs):
        return tuple(Slope(blocks, ref, *coefficients[4 * n:4 * n + 4]) for ref in refs)

    def one_step():
        first, second = slopes_of(0, e, g), slopes_of(1, e1, g1)

        def finish(k):
            e1[k], g1[k] = first[0].divergence(k), first[1].divergence(k)

        def finish_step(k):
            parts = (e[k], g[k], e1[k], g1[k], second[0].divergence(k), second[1].divergence(k))
            total_e[k] = DAMP * total_e[k] + parts[0] + weighted(W_MIX[1:4], parts[1:4])
            e[k] = (parts[0] + parts[1]) + (parts[2] + parts[4]) + E_MIX * parts[3]
            g[k] = weighted(G_MIX, parts)

        return [(first, finish), (second, finish_step)]

    def some_steps(_, carry):
        emit(blocks, [sweep for _ in range(UNROLL) for sweep in one_step()])
        return carry

    lax.fori_loop(0, STEPS // UNROLL, some_steps, 0)

    def square(k):
        depth = rows[2, strided(k), :]
        return depth * depth * (GRAVITY / 3.0 * W_SCALE)

    a = Memo(lambda k: -0.5 * GRAVITY * W_SCALE + 2.0 * square(k))
    b = Memo(lambda k: -0.5 * square(k))
    a_east, b_east = Memo(lambda k: turned(a[k], -1, 1)), Memo(lambda k: turned(b[k], -1, 1))
    slope = Slope(blocks, total_e, a, b, a_east, b_east, diverge=False)

    def finish_velocity(k):
        rows[0, strided(k), :] = e[k]
        rows[1, strided(k), :] = slope.x_west[k]
        rows[2, strided(k), :] = slope.y[k]

    emit(blocks, [((slope,), finish_velocity)])

    def tile(f):
        return rows[f, HALO:HALO + length].T[HALO:HALO + out_e.shape[0]]

    wet = own[3] > 0.0
    out_e[...] = tile(0)
    for out, flow, f in ((out_x, flow_x, 1), (out_y, flow_y, 2)):
        before = flow[...]
        out[...] = jnp.where(wet, DAMP**STEPS * before + tile(f), before)


def on_device(surface, velocity_x, velocity_y, classes, wet_mask):
    width, length = surface.shape
    wet = wet_mask.astype(jnp.float32)
    depth = (0.15 + classes.astype(jnp.float32) * (0.4 / 7.0)) * wet
    own = jnp.stack([surface, depth * velocity_x, depth * velocity_y, depth])
    rest = HALO - width
    got_1, got_2, got_3 = (move(own, "gx", steps) for steps in MOVES[:3])
    got_4 = move(own[:, :rest], "gx", MOVES[3])
    lanes = width + 2 * HALO
    f32 = jnp.float32
    packet = jax.ShapeDtypeStruct((3 * (FULL + ROW) + ROW, lanes), f32)
    centre, to_outer, to_inner, ends = pl.pallas_call(
        gather_kernel,
        out_shape=(
            jax.ShapeDtypeStruct((3, length, lanes), f32),
            packet,
            packet,
            jax.ShapeDtypeStruct((2 * ROW, lanes), f32),
        ),
        scratch_shapes=[pltpu.VMEM(packet.shape, f32)] * 2,
        compiler_params=pltpu.CompilerParams(vmem_limit_bytes=VMEM_LIMIT),
        name="turn",
    )(got_4, got_3, got_2, got_1, own)
    inner = move(to_inner, "gy", INNER)
    outer = move(to_outer, "gy", OUTER)
    total = length + 2 * HALO
    blocked = pltpu.VMEM((total // ROW, ROW, lanes), f32)
    return pl.pallas_call(
        step_kernel,
        out_shape=tuple(jax.ShapeDtypeStruct((width, length), f32) for _ in range(3)),
        scratch_shapes=[pltpu.VMEM((3, total, lanes), f32)] + [pltpu.VMEM(packet.shape, f32)] * 2 + [blocked] * 13,
        compiler_params=pltpu.CompilerParams(vmem_limit_bytes=VMEM_LIMIT),
        name="steps",
    )(outer, inner, centre, ends, own, velocity_x, velocity_y)


def solution(mesh):
    return jax.shard_map(
        on_device,
        mesh=mesh,
        in_specs=(P("gx", "gy"),) * 5,
        out_specs=(P("gx", "gy"),) * 3,
        check_vma=False,
    )
```

time: 363 us -> 23.4 us (0.06)
  starting transfers between devices: 221 us -> 10.2 us
  waiting for transfers between devices: 109 us -> 4.39 us
  other arithmetic: 19.3 us -> 0.79 us
  local copies, waits for them, and re-layouts: 8.95 us -> 0.01 us
  Pallas kernels: 0 us -> 7.08 us
    ppermute x132 -> x6, starting transfers between devices: 221 us -> 10.2 us  [move(): lax.ppermute(cells, axis, [(i, (i + steps[i % len(steps)]) % count) for i...]
    ppermute x132 -> x6, waiting for transfers between devices: 109 us -> 4.39 us  [move(): lax.ppermute(cells, axis, [(i, (i + steps[i % len(steps)]) % count) for i...]
    slice x129 -> x1, local copies, waits for them, and re-layouts: 7.98 us -> 0.01 us  [on_device(): got_4 = move(own[:, :rest], 'gx', MOVES[3])]
    pallas_call x0 -> x2, Pallas kernels: none -> 7.08 us  [the longest x1 6.84 us: on_device(): pl.pallas_call(step_kernel, out_shape=tuple((jax.ShapeDtypeStruct((width,...]
    another operation x66 -> x2, other arithmetic: 6.46 us -> 0.79 us  [on_device(): own = jnp.stack([surface, depth * velocity_x, depth * velocity_y, depth])]
    concatenate x65 -> x0, other arithmetic: 4.47 us -> none  [padded_2(): jnp.concatenate([lax.ppermute(tail, axis, [(i, (i + 1) % count) for i in...]
    add x32 -> x0, other arithmetic: 3.66 us -> none  [the longest x8 1.03 us: on_device(): state + TIME_STEP / 6.0 * (first + 2.0 * second + 2.0 * third + fourth)]
  transfers between devices with their start and end apart: 132 -> 6, of which waited for: 65 -> 3; matrix products, arithmetic and copies ran while one was open for 0% -> 0% of each run, Pallas kernels for 0% -> 0%
where the time goes in v1:
time: 23.4 us; the launch traced here: 23.1 us
  starting transfers between devices  10.2 us (44%)
  Pallas kernels  7.08 us (30%)
  waiting for transfers between devices  4.39 us (19%)
  other arithmetic  0.79 us (3%)
  between operations  0.67 us (3%)
    ppermute x6, starting transfers between devices, move(): lax.ppermute(cells, axis, [(i, (i + steps[i % len(steps)]) % count) for i...  10.2 us
    pallas_call x1, Pallas kernels, on_device(): pl.pallas_call(step_kernel, out_shape=tuple((jax.ShapeDtypeStruct((width,...  6.84 us
    ppermute x6, waiting for transfers between devices, move(): lax.ppermute(cells, axis, [(i, (i + steps[i % len(steps)]) % count) for i...  4.39 us
    another operation x2, other arithmetic, on_device(): own = jnp.stack([surface, depth * velocity_x, depth * velocity_y, depth])  0.79 us
  transfers between devices with their start and end apart: 6, of which 3 were waited for; matrix products, arithmetic and copies ran while one was open for 0% of the time, Pallas kernels for 0%

profile of v1, /device:TPU:0, one launch (start us, length us, event | category | flops | bytes accessed | tf_op | source)
XLA Modules:
  0.0 23.1 jit_solution(4860011895514810322)
XLA Ops:
  0.6 0.0 copy-start.2
  0.6 0.8 %multiply_bitcast_fusion.1 = (f32[1,32,128]{2,1,0:T(8,128)S(1)}, f32[1,32,128]{2,1,0:T(8,128)S(1)}, f32[1,32,128]{2,1,0:T(8,128)S(1)}) fusion(f32[32,128]{1,0:T(8,128)} %flow_x.1, s32[32,128]{1,0:T(8,128)} %param.9, s32[32,128]{1,0:T(8,128)} %param.8, f32[32,128]{1,0:T(8,128)} %flow_y.1), kind=kLoop, calls=%fused_computation.2 | loop fusion | flops 28672 | bytes 114688 | tf_op jit(solution)/shard_map/stack | solution.py:326
  1.4 0.0 copy-done.2
  1.5 3.1 %collective-permute-start.3 = (f32[4,32,128]{2,1,0:T(8,128)S(1)}, f32[4,32,128]{2,1,0:T(8,128)S(1)}, u32[]{:S(2)}, u32[]{:S(2)}) collective-permute-start(f32[4,32,128]{2,1,0:T(8,128)S(1)} %pad_maximum_fusion.own), channel_id=1, source_target_pairs={{0,8},{4,12},{8,4},{12,16},{16,24},{20,28},{24,20},{28,0},{1,9},{5... | collective-permute-start | bytes 196616 | tf_op jit(solution)/shard_map/ppermute | solution.py:55
  4.5 3.0 %collective-permute-start.2 = (f32[4,32,128]{2,1,0:T(8,128)S(1)}, f32[4,32,128]{2,1,0:T(8,128)S(1)}, u32[]{:S(2)}, u32[]{:S(2)}) collective-permute-start(f32[4,32,128]{2,1,0:T(8,128)S(1)} %pad_maximum_fusion.own), channel_id=1, source_target_pairs={{0,28},{4,8},{8,16},{12,20},{16,12},{20,24},{24,0},{28,4},{1,29},{... | collective-permute-start | bytes 196616 | tf_op jit(solution)/shard_map/ppermute | solution.py:55
  7.5 0.0 collective-permute-start.1
  7.6 2.3 %collective-permute-start = (f32[4,16,128]{2,1,0:T(8,128)S(1)}, f32[4,16,128]{2,1,0:T(8,128)S(1)}, u32[]{:S(2)}, u32[]{:S(2)}) collective-permute-start(f32[4,16,128]{2,1,0:T(8,128)S(1)} %slice.4), channel_id=1, source_target_pairs={{0,24},{4,28},{8,0},{12,4},{16,8},{20,12},{24,16},{28,20},{1,25},{... | collective-permute-start | bytes 98312 | tf_op jit(solution)/shard_map/ppermute | solution.py:55
  9.8 1.7 %collective-permute-done.got_4 = f32[4,16,128]{2,1,0:T(8,128)S(1)} collective-permute-done((f32[4,16,128]{2,1,0:T(8,128)S(1)}, f32[4,16,128]{2,1,0:T(8,128)S(1)}, u32[]{:S(2)}, u32[]{:S(2)}) %collective-permute-start) | collective-permute-done | bytes 32800 | tf_op jit(solution)/shard_map/ppermute | solution.py:55
  11.6 0.0 collective-permute-done.3.got_1
  11.6 0.0 collective-permute-done.2.got_2
  11.6 0.2 collective-permute-done.1.got_3
  11.8 0.0 copy-start
  11.8 0.0 copy-start.1
  11.8 0.2 %turn.1 = (f32[3,128,128]{2,1,0:T(8,128)S(1)}, f32[128,128]{1,0:T(8,128)S(1)}, f32[128,128]{1,0:T(8,128)S(1)}, f32[16,128]{1,0:T(8,128)S(1)}) custom-call(f32[4,16,128]{2,1,0:T(8,128)S(1)} %collective-permute-done.got_4, f32[4,32,128]{2,1,0:T(8,128)S(1)} %collective-permute-done.1.got_3, f32[4,32,128]{2,1,0:T(8,128)S(1)} %collective-permute-done.2.got_2, ...), custom_call_target="tpu_custom_call" | custom-call | tf_op jit(solution)/shard_map/turn/pallas_call | solution.py:333
  12.1 0.2 %collective-permute-start.4 = (f32[128,128]{1,0:T(8,128)S(1)}, f32[128,128]{1,0:T(8,128)S(1)}, u32[]{:S(2)}, u32[]{:S(2)}) collective-permute-start(f32[128,128]{1,0:T(8,128)S(1)} %get-tuple-element.7), channel_id=1, source_target_pairs={{0,3},{1,2},{2,1},{3,0},{4,7},{5,6},{6,5},{7,4},{8,11},{9,10},{10,... | collective-permute-start | bytes 196616 | tf_op jit(solution)/shard_map/ppermute | solution.py:55
  12.3 1.6 %collective-permute-start.5 = (f32[128,128]{1,0:T(8,128)S(1)}, f32[128,128]{1,0:T(8,128)S(1)}, u32[]{:S(2)}, u32[]{:S(2)}) collective-permute-start(f32[128,128]{1,0:T(8,128)S(1)} %get-tuple-element.8), channel_id=1, source_target_pairs={{0,1},{1,0},{2,3},{3,2},{4,5},{5,4},{6,7},{7,6},{8,9},{9,8},{10,11... | collective-permute-start | bytes 196616 | tf_op jit(solution)/shard_map/ppermute | solution.py:55
  13.9 2.4 %collective-permute-done.4.outer = f32[128,128]{1,0:T(8,128)S(1)} collective-permute-done((f32[128,128]{1,0:T(8,128)S(1)}, f32[128,128]{1,0:T(8,128)S(1)}, u32[]{:S(2)}, u32[]{:S(2)}) %collective-permute-start.4) | collective-permute-done | bytes 65568 | tf_op jit(solution)/shard_map/ppermute | solution.py:55
  16.3 0.0 collective-permute-done.5.inner
  16.3 0.0 copy-done
  16.3 0.0 copy-done.1
  16.3 6.8 %steps.1 = (f32[32,128]{1,0:T(8,128)}, f32[32,128]{1,0:T(8,128)}, f32[32,128]{1,0:T(8,128)}) custom-call(f32[128,128]{1,0:T(8,128)S(1)} %collective-permute-done.4.outer, f32[128,128]{1,0:T(8,128)S(1)} %collective-permute-done.5.inner, f32[3,128,128]{2,1,0:T(8,128)S(1)} %get-tuple-element.9.centre, f32[16,128]{1,0:T(8,128)S(1)} %get-tuple-element.10.ends, ...), custom_call_target="tpu_custom_call" | custom-call | tf_op jit(solution)/shard_map/steps/pallas_call | solution.py:349
  (2 shorter events, 0.0 us)
Async XLA Ops:
  0.6 0.8 %copy-start.2 = (f32[32,128]{1,0:T(8,128)S(1)}, f32[32,128]{1,0:T(8,128)}, u32[]{:S(2)}) copy-start(f32[32,128]{1,0:T(8,128)} %param.5) | copy-start | bytes 49156
  1.5 10.1 %collective-permute-start.3 = (f32[4,32,128]{2,1,0:T(8,128)S(1)}, f32[4,32,128]{2,1,0:T(8,128)S(1)}, u32[]{:S(2)}, u32[]{:S(2)}) collective-permute-start(f32[4,32,128]{2,1,0:T(8,128)S(1)} %pad_maximum_fusion.own), channel_id=1, source_target_pairs={{0,8},{4,12},{8,4},{12,16},{16,24},{20,28},{24,20},{28,0},{1,9},{5... | collective-permute-start | bytes 196616 | tf_op jit(solution)/shard_map/ppermute | solution.py:55
  4.5 7.1 %collective-permute-start.2 = (f32[4,32,128]{2,1,0:T(8,128)S(1)}, f32[4,32,128]{2,1,0:T(8,128)S(1)}, u32[]{:S(2)}, u32[]{:S(2)}) collective-permute-start(f32[4,32,128]{2,1,0:T(8,128)S(1)} %pad_maximum_fusion.own), channel_id=1, source_target_pairs={{0,28},{4,8},{8,16},{12,20},{16,12},{20,24},{24,0},{28,4},{1,29},{... | collective-permute-start | bytes 196616 | tf_op jit(solution)/shard_map/ppermute | solution.py:55
  7.5 4.3 %collective-permute-start.1 = (f32[4,32,128]{2,1,0:T(8,128)S(1)}, f32[4,32,128]{2,1,0:T(8,128)S(1)}, u32[]{:S(2)}, u32[]{:S(2)}) collective-permute-start(f32[4,32,128]{2,1,0:T(8,128)S(1)} %pad_maximum_fusion.own), channel_id=1, source_target_pairs={{0,4},{4,0},{8,12},{12,8},{16,20},{20,16},{24,28},{28,24},{1,5},{5... | collective-permute-start | bytes 196616 | tf_op jit(solution)/shard_map/ppermute | solution.py:55
  7.6 4.0 %collective-permute-start = (f32[4,16,128]{2,1,0:T(8,128)S(1)}, f32[4,16,128]{2,1,0:T(8,128)S(1)}, u32[]{:S(2)}, u32[]{:S(2)}) collective-permute-start(f32[4,16,128]{2,1,0:T(8,128)S(1)} %slice.4), channel_id=1, source_target_pairs={{0,24},{4,28},{8,0},{12,4},{16,8},{20,12},{24,16},{28,20},{1,25},{... | collective-permute-start | bytes 98312 | tf_op jit(solution)/shard_map/ppermute | solution.py:55
  11.8 4.5 %copy-start = (f32[32,128]{1,0:T(8,128)S(1)}, f32[32,128]{1,0:T(8,128)}, u32[]{:S(2)}) copy-start(f32[32,128]{1,0:T(8,128)} %flow_x.1) | copy-start | bytes 49156
  11.8 4.5 %copy-start.1 = (f32[32,128]{1,0:T(8,128)S(1)}, f32[32,128]{1,0:T(8,128)}, u32[]{:S(2)}) copy-start(f32[32,128]{1,0:T(8,128)} %flow_y.1) | copy-start | bytes 49156
  12.1 4.2 %collective-permute-start.4 = (f32[128,128]{1,0:T(8,128)S(1)}, f32[128,128]{1,0:T(8,128)S(1)}, u32[]{:S(2)}, u32[]{:S(2)}) collective-permute-start(f32[128,128]{1,0:T(8,128)S(1)} %get-tuple-element.7), channel_id=1, source_target_pairs={{0,3},{1,2},{2,1},{3,0},{4,7},{5,6},{6,5},{7,4},{8,11},{9,10},{10,... | collective-permute-start | bytes 196616 | tf_op jit(solution)/shard_map/ppermute | solution.py:55
  12.3 4.0 %collective-permute-start.5 = (f32[128,128]{1,0:T(8,128)S(1)}, f32[128,128]{1,0:T(8,128)S(1)}, u32[]{:S(2)}, u32[]{:S(2)}) collective-permute-start(f32[128,128]{1,0:T(8,128)S(1)} %get-tuple-element.8), channel_id=1, source_target_pairs={{0,1},{1,0},{2,3},{3,2},{4,5},{5,4},{6,7},{7,6},{8,9},{9,8},{10,11... | collective-permute-start | bytes 196616 | tf_op jit(solution)/shard_map/ppermute | solution.py:55

commit v2 on v1

--- a/solution.py
+++ b/solution.py
@@ -17,10 +17,9 @@
 HALO = 3 * 2 * STEPS
 ROW = 8
 FULL = 32
-AHEAD = 5
-LAG = 8
-SEAM = 2
-UNROLL = 2
+MOVE = 6
+LAST = 2
+UNROLL = 1
 VMEM_LIMIT = 8 * 1024 * 1024
 
 R = FRICTION
@@ -127,7 +126,7 @@
 
 class Rows:
     def __init__(self, blocks, source):
-        self.blocks, self.source = blocks, source
+        self.blocks, self.source, self.seam = blocks, source, {}
 
     def __getitem__(self, k):
         return self.source[k]
@@ -135,14 +134,36 @@
     def __setitem__(self, k, value):
         self.source[k] = value
 
+    def over_seam(self, k):
+        if k not in self.seam:
+            self.seam[k] = turned(self[k], -1 if k == 0 else 1, 0)
+        return self.seam[k]
+
     def north(self, k):
-        return self[k + 1] if k < self.blocks - 1 else turned(self[0], -1, 0)
+        return self[k + 1] if k < self.blocks - 1 else self.over_seam(0)
 
     def south(self, k):
-        return self[k - 1] if k > 0 else turned(self[self.blocks - 1], 1, 0)
+        return self[k - 1] if k > 0 else self.over_seam(self.blocks - 1)
 
 
 class Slope:
+    AHEAD, LAG, SEAM = 5, 8, 2
+    EDGE = ("slope_y",)
+
+    @classmethod
+    def parts(cls):
+        top = 2 * cls.AHEAD
+        assert 4 + 2 * cls.SEAM <= cls.LAG
+        return (
+            ("finish", top + 2 * cls.LAG, 2),
+            ("sum_up", top, 0),
+            ("slope_y", top + 2, 1),
+            ("lift_y", top + 4, 2),
+            ("slope_x", top + cls.LAG, 2),
+            ("rotate_sum", cls.AHEAD, 0),
+            ("rotate", 0, 0),
+        )
+
     def __init__(self, blocks, ref, alpha, beta, alpha_east, beta_east, diverge=True):
         self.field = Rows(blocks, ref)
         self.alpha, self.beta, self.alpha_east, self.beta_east = alpha, beta, alpha_east, beta_east
@@ -184,6 +205,67 @@
         return self.wait.pop(k) - self.x_west.pop(k)
 
 
+class QuickSlope:
+    AHEAD, LAG, SEAM = 6, 6, 2
+    EDGE = ("slope_x", "slope_y")
+
+    @classmethod
+    def parts(cls):
+        assert 1 + 2 * cls.SEAM <= cls.LAG
+        return (
+            ("finish", cls.AHEAD + 3 + cls.LAG, 2),
+            ("sum_up", cls.AHEAD, 0),
+            ("slope_x", cls.AHEAD + 2, 1),
+            ("slope_y", cls.AHEAD + 2, 1),
+            ("lift_y", cls.AHEAD + 4, 2),
+            ("rotate", 0, 0),
+        )
+
+    def __init__(self, blocks, ref, alpha, beta, alpha_east, beta_east, diverge=True):
+        self.blocks, self.diverge = blocks, diverge
+        self.alpha, self.beta, self.alpha_east, self.beta_east = alpha, beta, alpha_east, beta_east
+        self.field = Rows(blocks, ref)
+        self.at, self.far, self.dx, self.dy, self.x, self.x_west = {}, {}, {}, {}, {}, {}
+        self.east_2, self.sums, self.y = (Rows(blocks, {}) for _ in range(3))
+
+    def rotate(self, k):
+        here = self.field[k]
+        self.at[k] = tuple(turned(here, by, 1) for by in (-1, 1, -3))
+        self.east_2[k] = turned(here, -2, 1)
+        if k in (0, self.blocks - 1):
+            self.field.over_seam(k)
+
+    def sum_up(self, k):
+        east_1, west_1, east_3 = self.at.pop(k)
+        north, south = self.field.north(k), self.field.south(k)
+        self.dy[k] = north - south
+        self.sums[k] = (east_1 + west_1) + (north + south)
+        self.far[k] = east_3 + east_1
+        self.dx[k] = self.east_2[k] - self.field[k]
+        if k in (0, self.blocks - 1):
+            self.sums.over_seam(k)
+            self.east_2.over_seam(k)
+
+    def slope_x(self, k):
+        sums_east = self.far.pop(k) + (self.east_2.north(k) + self.east_2.south(k))
+        x = self.alpha_east[k] * self.dx.pop(k) + self.beta_east[k] * (sums_east - self.sums[k])
+        self.x[k] = x
+        self.x_west[k] = turned(x, 2 if self.diverge else 1, 1)
+
+    def slope_y(self, k):
+        s = self.sums
+        self.y[k] = self.alpha[k] * self.dy.pop(k) + self.beta[k] * (s.north(k) - s.south(k))
+        if k in (0, self.blocks - 1):
+            self.y.over_seam(k)
+
+    def lift_y(self, k):
+        if self.diverge:
+            self.x[k] = self.x[k] + (self.y.north(k) - self.y.south(k))
+
+    def divergence(self, k):
+        return self.x.pop(k) - self.x_west.pop(k)
+
+
 class Memo:
     def __init__(self, make):
         self.make, self.made = make, {}
@@ -194,32 +276,19 @@
         return self.made[k]
 
 
-def parts_of(blocks):
-    top = 2 * AHEAD
-    assert top + 2 * LAG <= blocks - 2 and 4 + 2 * SEAM <= LAG
-    return (
-        ("finish", top + 2 * LAG, 2),
-        ("sum_up", top, 0),
-        ("slope_y", top + 2, 1),
-        ("lift_y", top + 4, 2),
-        ("slope_x", top + LAG, 2),
-        ("rotate_sum", AHEAD, 0),
-        ("rotate", 0, 0),
-    )
-
-
 def emit(blocks, sweeps):
-    edge = {
-        "slope_y": {0: 1, blocks - 1: 1},
-        "lift_y": {0: 2, blocks - 1: 2, 1: 1, blocks - 2: 1},
-    }
-    parts = parts_of(blocks)
+    kind = type(sweeps[0][0][0])
+    seam = kind.SEAM
+    edge = {name: {0: seam, blocks - 1: seam} for name in kind.EDGE}
+    edge["lift_y"] = {0: 2 * seam, blocks - 1: 2 * seam, 1: seam, blocks - 2: seam}
+    parts = kind.parts()
+    every = max(blocks, parts[0][1] + 1)
     slots = {}
-    for number, (slopes, finish) in enumerate(sweeps):
+    for number in range(len(sweeps)):
         for order, (name, begin, ahead) in enumerate(parts):
             for i in range(blocks):
                 k = (i + ahead + 3 * number) % blocks
-                slot = number * blocks + begin + i + SEAM * edge.get(name, {}).get(k, 0)
+                slot = number * every + begin + i + edge.get(name, {}).get(k, 0)
                 slots.setdefault(slot, []).append((number, order, name, k))
     for slot in sorted(slots):
         for number, _, name, k in sorted(slots[slot]):
@@ -232,7 +301,7 @@
 
 
 def step_kernel(outer, inner, centre, ends, own, flow_x, flow_y, out_e, out_x, out_y,
-                rows, low, high, e, g, e1, g1, total_e, *coefficients):
+                rows, low, high, kept, e, g, e1, g1, total_e, *coefficients):
     length = centre.shape[1]
     total = length + 2 * HALO
     blocks = total // ROW
@@ -258,11 +327,7 @@
     def strided(k):
         return pl.ds(k, ROW, stride=blocks)
 
-    for k in range(blocks):
-        e[k] = rows[0, strided(k), :]
-        g[k] = rows[1, strided(k), :]
-        total_e[k] = jnp.zeros((ROW, e.shape[2]), jnp.float32)
-        depth = rows[2, strided(k), :]
+    def set_coefficients(k, depth):
         cube = depth * depth * depth * (GRAVITY / 12.0)
         slow = 0.25 * GRAVITY * depth - 4.0 * cube
         both = (slow, cube, turned(slow, -1, 1), turned(cube, -1, 1))
@@ -270,11 +335,17 @@
             for ref, value in zip(coefficients[4 * n:4 * n + 4], both):
                 ref[k] = K_SCALE[n] * value
 
-    def slopes_of(n, *refs):
-        return tuple(Slope(blocks, ref, *coefficients[4 * n:4 * n + 4]) for ref in refs)
-
-    def one_step():
-        first, second = slopes_of(0, e, g), slopes_of(1, e1, g1)
+    for k in range(blocks):
+        e[k] = rows[0, strided(k), :]
+        g[k] = rows[1, strided(k), :]
+        total_e[k] = jnp.zeros((ROW, e.shape[2]), jnp.float32)
+        set_coefficients(k, rows[2, strided(k), :])
+
+    def one_step(kind, count):
+        first, second = (
+            tuple(kind(count, ref, *coefficients[4 * n:4 * n + 4]) for ref in refs)
+            for n, refs in enumerate(((e, g), (e1, g1)))
+        )
 
         def finish(k):
             e1[k], g1[k] = first[0].divergence(k), first[1].divergence(k)
@@ -288,29 +359,54 @@
         return [(first, finish), (second, finish_step)]
 
     def some_steps(_, carry):
-        emit(blocks, [sweep for _ in range(UNROLL) for sweep in one_step()])
+        emit(blocks, [sweep for _ in range(UNROLL) for sweep in one_step(Slope, blocks)])
         return carry
 
-    lax.fori_loop(0, STEPS // UNROLL, some_steps, 0)
-
-    def square(k):
-        depth = rows[2, strided(k), :]
-        return depth * depth * (GRAVITY / 3.0 * W_SCALE)
-
-    a = Memo(lambda k: -0.5 * GRAVITY * W_SCALE + 2.0 * square(k))
-    b = Memo(lambda k: -0.5 * square(k))
+    lax.fori_loop(0, (STEPS - LAST) // UNROLL, some_steps, 0)
+
+    margin, half = MOVE * LAST, length // 2
+    few = (half + 2 * margin) // ROW
+    for f, ref in ((0, e), (1, g), (3, total_e)):
+        for k in range(blocks):
+            rows[f, strided(k), :] = ref[k]
+
+    def folded(f, k):
+        first, second = (
+            rows[f, pl.ds(HALO - margin + start + k, ROW, stride=few), :] for start in (0, half)
+        )
+        return fold(first, second)
+
+    for k in range(few):
+        e[k], g[k], total_e[k], kept[k] = (folded(f, k) for f in (0, 1, 3, 2))
+        set_coefficients(k, kept[k])
+
+    def last_step(_, carry):
+        emit(few, one_step(QuickSlope, few))
+        return carry
+
+    lax.fori_loop(0, LAST, last_step, 0)
+
+    square = Memo(lambda k: kept[k] * kept[k] * (GRAVITY / 3.0 * W_SCALE))
+    a = Memo(lambda k: -0.5 * GRAVITY * W_SCALE + 2.0 * square[k])
+    b = Memo(lambda k: -0.5 * square[k])
     a_east, b_east = Memo(lambda k: turned(a[k], -1, 1)), Memo(lambda k: turned(b[k], -1, 1))
-    slope = Slope(blocks, total_e, a, b, a_east, b_east, diverge=False)
+    slope = QuickSlope(few, total_e, a, b, a_east, b_east, diverge=False)
 
     def finish_velocity(k):
-        rows[0, strided(k), :] = e[k]
-        rows[1, strided(k), :] = slope.x_west[k]
-        rows[2, strided(k), :] = slope.y[k]
-
-    emit(blocks, [((slope,), finish_velocity)])
+        at = pl.ds(k, ROW, stride=few)
+        rows[0, at, :] = e[k]
+        rows[1, at, :] = slope.x_west[k]
+        rows[2, at, :] = slope.y[k]
+
+    emit(few, [((slope,), finish_velocity)])
 
     def tile(f):
-        return rows[f, HALO:HALO + length].T[HALO:HALO + out_e.shape[0]]
+        width = out_e.shape[0]
+        both = rows[f, margin:margin + length].T
+        first = HALO - 32
+        low_rows, high_rows = both[first:first + width], both[64 + first:64 + first + width]
+        lane = lax.broadcasted_iota(jnp.int32, low_rows.shape, 1)
+        return jnp.where(lane < half, low_rows, pltpu.roll(high_rows, half, 1))
 
     wet = own[3] > 0.0
     out_e[...] = tile(0)
@@ -349,7 +445,7 @@
     return pl.pallas_call(
         step_kernel,
         out_shape=tuple(jax.ShapeDtypeStruct((width, length), f32) for _ in range(3)),
-        scratch_shapes=[pltpu.VMEM((3, total, lanes), f32)] + [pltpu.VMEM(packet.shape, f32)] * 2 + [blocked] * 13,
+        scratch_shapes=[pltpu.VMEM((4, total, lanes), f32)] + [pltpu.VMEM(packet.shape, f32)] * 2 + [blocked] * 14,
         compiler_params=pltpu.CompilerParams(vmem_limit_bytes=VMEM_LIMIT),
         name="steps",
     )(outer, inner, centre, ends, own, velocity_x, velocity_y)

time: 23.4 us -> 24.1 us (1.030)
  Pallas kernels: 7.08 us -> 7.73 us
    pallas_call x1, Pallas kernels: 6.84 us -> 7.49 us  [on_device(): pl.pallas_call(step_kernel, out_shape=tuple((jax.ShapeDtypeStruct((width,...]
where the time goes in v2:
time: 24.1 us; the launch traced here: 23.8 us
  starting transfers between devices  10.2 us (42%)
  Pallas kernels  7.73 us (32%)
  waiting for transfers between devices  4.39 us (18%)
  other arithmetic  0.79 us (3%)
  between operations  0.67 us (3%)
    ppermute x6, starting transfers between devices, move(): lax.ppermute(cells, axis, [(i, (i + steps[i % len(steps)]) % count) for i...  10.2 us
    pallas_call x1, Pallas kernels, on_device(): pl.pallas_call(step_kernel, out_shape=tuple((jax.ShapeDtypeStruct((width,...  7.49 us
    ppermute x6, waiting for transfers between devices, move(): lax.ppermute(cells, axis, [(i, (i + steps[i % len(steps)]) % count) for i...  4.39 us
    another operation x2, other arithmetic, on_device(): own = jnp.stack([surface, depth * velocity_x, depth * velocity_y, depth])  0.79 us
  transfers between devices with their start and end apart: 6, of which 3 were waited for; matrix products, arithmetic and copies ran while one was open for 0% of the time, Pallas kernels for 0%

profile of v2, /device:TPU:0, one launch (start us, length us, event | category | flops | bytes accessed | tf_op | source)
XLA Modules:
  0.0 23.8 jit_solution(11552431978543360226)
XLA Ops:
  0.6 0.0 copy-start.2
  0.6 0.8 %multiply_bitcast_fusion.1 = (f32[1,32,128]{2,1,0:T(8,128)S(1)}, f32[1,32,128]{2,1,0:T(8,128)S(1)}, f32[1,32,128]{2,1,0:T(8,128)S(1)}) fusion(f32[32,128]{1,0:T(8,128)} %flow_x.1, s32[32,128]{1,0:T(8,128)} %param.9, s32[32,128]{1,0:T(8,128)} %param.8, f32[32,128]{1,0:T(8,128)} %flow_y.1), kind=kLoop, calls=%fused_computation.2 | loop fusion | flops 28672 | bytes 114688 | tf_op jit(solution)/shard_map/stack | solution.py:422
  1.4 0.0 copy-done.2
  1.5 3.1 %collective-permute-start.3 = (f32[4,32,128]{2,1,0:T(8,128)S(1)}, f32[4,32,128]{2,1,0:T(8,128)S(1)}, u32[]{:S(2)}, u32[]{:S(2)}) collective-permute-start(f32[4,32,128]{2,1,0:T(8,128)S(1)} %pad_maximum_fusion.own), channel_id=1, source_target_pairs={{0,8},{4,12},{8,4},{12,16},{16,24},{20,28},{24,20},{28,0},{1,9},{5... | collective-permute-start | bytes 196616 | tf_op jit(solution)/shard_map/ppermute | solution.py:54
  4.5 3.0 %collective-permute-start.2 = (f32[4,32,128]{2,1,0:T(8,128)S(1)}, f32[4,32,128]{2,1,0:T(8,128)S(1)}, u32[]{:S(2)}, u32[]{:S(2)}) collective-permute-start(f32[4,32,128]{2,1,0:T(8,128)S(1)} %pad_maximum_fusion.own), channel_id=1, source_target_pairs={{0,28},{4,8},{8,16},{12,20},{16,12},{20,24},{24,0},{28,4},{1,29},{... | collective-permute-start | bytes 196616 | tf_op jit(solution)/shard_map/ppermute | solution.py:54
  7.5 0.0 collective-permute-start.1
  7.6 2.3 %collective-permute-start = (f32[4,16,128]{2,1,0:T(8,128)S(1)}, f32[4,16,128]{2,1,0:T(8,128)S(1)}, u32[]{:S(2)}, u32[]{:S(2)}) collective-permute-start(f32[4,16,128]{2,1,0:T(8,128)S(1)} %slice.4), channel_id=1, source_target_pairs={{0,24},{4,28},{8,0},{12,4},{16,8},{20,12},{24,16},{28,20},{1,25},{... | collective-permute-start | bytes 98312 | tf_op jit(solution)/shard_map/ppermute | solution.py:54
  9.8 1.7 %collective-permute-done.got_4 = f32[4,16,128]{2,1,0:T(8,128)S(1)} collective-permute-done((f32[4,16,128]{2,1,0:T(8,128)S(1)}, f32[4,16,128]{2,1,0:T(8,128)S(1)}, u32[]{:S(2)}, u32[]{:S(2)}) %collective-permute-start) | collective-permute-done | bytes 32800 | tf_op jit(solution)/shard_map/ppermute | solution.py:54
  11.6 0.0 collective-permute-done.3.got_1
  11.6 0.0 collective-permute-done.2.got_2
  11.6 0.2 collective-permute-done.1.got_3
  11.8 0.0 copy-start
  11.8 0.0 copy-start.1
  11.8 0.2 %turn.1 = (f32[3,128,128]{2,1,0:T(8,128)S(1)}, f32[128,128]{1,0:T(8,128)S(1)}, f32[128,128]{1,0:T(8,128)S(1)}, f32[16,128]{1,0:T(8,128)S(1)}) custom-call(f32[4,16,128]{2,1,0:T(8,128)S(1)} %collective-permute-done.got_4, f32[4,32,128]{2,1,0:T(8,128)S(1)} %collective-permute-done.1.got_3, f32[4,32,128]{2,1,0:T(8,128)S(1)} %collective-permute-done.2.got_2, ...), custom_call_target="tpu_custom_call" | custom-call | tf_op jit(solution)/shard_map/turn/pallas_call | solution.py:429
  12.1 0.2 collective-permute-start.4
  12.3 1.6 %collective-permute-start.5 = (f32[128,128]{1,0:T(8,128)S(1)}, f32[128,128]{1,0:T(8,128)S(1)}, u32[]{:S(2)}, u32[]{:S(2)}) collective-permute-start(f32[128,128]{1,0:T(8,128)S(1)} %get-tuple-element.8), channel_id=1, source_target_pairs={{0,1},{1,0},{2,3},{3,2},{4,5},{5,4},{6,7},{7,6},{8,9},{9,8},{10,11... | collective-permute-start | bytes 196616 | tf_op jit(solution)/shard_map/ppermute | solution.py:54
  13.9 2.4 %collective-permute-done.4.outer = f32[128,128]{1,0:T(8,128)S(1)} collective-permute-done((f32[128,128]{1,0:T(8,128)S(1)}, f32[128,128]{1,0:T(8,128)S(1)}, u32[]{:S(2)}, u32[]{:S(2)}) %collective-permute-start.4) | collective-permute-done | bytes 65568 | tf_op jit(solution)/shard_map/ppermute | solution.py:54
  16.3 0.0 collective-permute-done.5.inner
  16.3 0.0 copy-done
  16.3 0.0 copy-done.1
  16.3 7.5 %steps.1 = (f32[32,128]{1,0:T(8,128)}, f32[32,128]{1,0:T(8,128)}, f32[32,128]{1,0:T(8,128)}) custom-call(f32[128,128]{1,0:T(8,128)S(1)} %collective-permute-done.4.outer, f32[128,128]{1,0:T(8,128)S(1)} %collective-permute-done.5.inner, f32[3,128,128]{2,1,0:T(8,128)S(1)} %get-tuple-element.9.centre, f32[16,128]{1,0:T(8,128)S(1)} %get-tuple-element.10.ends, ...), custom_call_target="tpu_custom_call" | custom-call | tf_op jit(solution)/shard_map/steps/pallas_call | solution.py:445
  (2 shorter events, 0.0 us)
Async XLA Ops:
  0.6 0.8 %copy-start.2 = (f32[32,128]{1,0:T(8,128)S(1)}, f32[32,128]{1,0:T(8,128)}, u32[]{:S(2)}) copy-start(f32[32,128]{1,0:T(8,128)} %param.5) | copy-start | bytes 49156
  1.5 10.1 %collective-permute-start.3 = (f32[4,32,128]{2,1,0:T(8,128)S(1)}, f32[4,32,128]{2,1,0:T(8,128)S(1)}, u32[]{:S(2)}, u32[]{:S(2)}) collective-permute-start(f32[4,32,128]{2,1,0:T(8,128)S(1)} %pad_maximum_fusion.own), channel_id=1, source_target_pairs={{0,8},{4,12},{8,4},{12,16},{16,24},{20,28},{24,20},{28,0},{1,9},{5... | collective-permute-start | bytes 196616 | tf_op jit(solution)/shard_map/ppermute | solution.py:54
  4.5 7.1 %collective-permute-start.2 = (f32[4,32,128]{2,1,0:T(8,128)S(1)}, f32[4,32,128]{2,1,0:T(8,128)S(1)}, u32[]{:S(2)}, u32[]{:S(2)}) collective-permute-start(f32[4,32,128]{2,1,0:T(8,128)S(1)} %pad_maximum_fusion.own), channel_id=1, source_target_pairs={{0,28},{4,8},{8,16},{12,20},{16,12},{20,24},{24,0},{28,4},{1,29},{... | collective-permute-start | bytes 196616 | tf_op jit(solution)/shard_map/ppermute | solution.py:54
  7.5 4.3 %collective-permute-start.1 = (f32[4,32,128]{2,1,0:T(8,128)S(1)}, f32[4,32,128]{2,1,0:T(8,128)S(1)}, u32[]{:S(2)}, u32[]{:S(2)}) collective-permute-start(f32[4,32,128]{2,1,0:T(8,128)S(1)} %pad_maximum_fusion.own), channel_id=1, source_target_pairs={{0,4},{4,0},{8,12},{12,8},{16,20},{20,16},{24,28},{28,24},{1,5},{5... | collective-permute-start | bytes 196616 | tf_op jit(solution)/shard_map/ppermute | solution.py:54
  7.6 4.0 %collective-permute-start = (f32[4,16,128]{2,1,0:T(8,128)S(1)}, f32[4,16,128]{2,1,0:T(8,128)S(1)}, u32[]{:S(2)}, u32[]{:S(2)}) collective-permute-start(f32[4,16,128]{2,1,0:T(8,128)S(1)} %slice.4), channel_id=1, source_target_pairs={{0,24},{4,28},{8,0},{12,4},{16,8},{20,12},{24,16},{28,20},{1,25},{... | collective-permute-start | bytes 98312 | tf_op jit(solution)/shard_map/ppermute | solution.py:54
  11.8 4.5 %copy-start = (f32[32,128]{1,0:T(8,128)S(1)}, f32[32,128]{1,0:T(8,128)}, u32[]{:S(2)}) copy-start(f32[32,128]{1,0:T(8,128)} %flow_x.1) | copy-start | bytes 49156
  11.8 4.5 %copy-start.1 = (f32[32,128]{1,0:T(8,128)S(1)}, f32[32,128]{1,0:T(8,128)}, u32[]{:S(2)}) copy-start(f32[32,128]{1,0:T(8,128)} %flow_y.1) | copy-start | bytes 49156
  12.1 4.2 %collective-permute-start.4 = (f32[128,128]{1,0:T(8,128)S(1)}, f32[128,128]{1,0:T(8,128)S(1)}, u32[]{:S(2)}, u32[]{:S(2)}) collective-permute-start(f32[128,128]{1,0:T(8,128)S(1)} %get-tuple-element.7), channel_id=1, source_target_pairs={{0,3},{1,2},{2,1},{3,0},{4,7},{5,6},{6,5},{7,4},{8,11},{9,10},{10,... | collective-permute-start | bytes 196616 | tf_op jit(solution)/shard_map/ppermute | solution.py:54
  12.3 4.0 %collective-permute-start.5 = (f32[128,128]{1,0:T(8,128)S(1)}, f32[128,128]{1,0:T(8,128)S(1)}, u32[]{:S(2)}, u32[]{:S(2)}) collective-permute-start(f32[128,128]{1,0:T(8,128)S(1)} %get-tuple-element.8), channel_id=1, source_target_pairs={{0,1},{1,0},{2,3},{3,2},{4,5},{5,4},{6,7},{7,6},{8,9},{9,8},{10,11... | collective-permute-start | bytes 196616 | tf_op jit(solution)/shard_map/ppermute | solution.py:54

commit v3 on v2

--- a/solution.py
+++ b/solution.py
@@ -19,7 +19,7 @@
 FULL = 32
 MOVE = 6
 LAST = 2
-UNROLL = 1
+UNROLL = 3
 VMEM_LIMIT = 8 * 1024 * 1024
 
 R = FRICTION

time: 24.1 us -> 23.1 us (0.959)
  Pallas kernels: 7.73 us -> 6.78 us
    pallas_call x1, Pallas kernels: 7.49 us -> 6.53 us  [on_device(): pl.pallas_call(step_kernel, out_shape=tuple((jax.ShapeDtypeStruct((width,...]
where the time goes in v3:
time: 23.1 us; the launch traced here: 22.8 us
  starting transfers between devices  10.2 us (44%)
  Pallas kernels  6.78 us (29%)
  waiting for transfers between devices  4.39 us (19%)
  other arithmetic  0.79 us (3%)
  between operations  0.67 us (3%)
    ppermute x6, starting transfers between devices, move(): lax.ppermute(cells, axis, [(i, (i + steps[i % len(steps)]) % count) for i...  10.2 us
    pallas_call x1, Pallas kernels, on_device(): pl.pallas_call(step_kernel, out_shape=tuple((jax.ShapeDtypeStruct((width,...  6.53 us
    ppermute x6, waiting for transfers between devices, move(): lax.ppermute(cells, axis, [(i, (i + steps[i % len(steps)]) % count) for i...  4.39 us
    another operation x2, other arithmetic, on_device(): own = jnp.stack([surface, depth * velocity_x, depth * velocity_y, depth])  0.79 us
  transfers between devices with their start and end apart: 6, of which 3 were waited for; matrix products, arithmetic and copies ran while one was open for 0% of the time, Pallas kernels for 0%

profile of v3, /device:TPU:0, one launch (start us, length us, event | category | flops | bytes accessed | tf_op | source)
XLA Modules:
  0.0 22.8 jit_solution(3288767422739087198)
XLA Ops:
  0.6 0.0 copy-start.2
  0.6 0.8 %multiply_bitcast_fusion.1 = (f32[1,32,128]{2,1,0:T(8,128)S(1)}, f32[1,32,128]{2,1,0:T(8,128)S(1)}, f32[1,32,128]{2,1,0:T(8,128)S(1)}) fusion(f32[32,128]{1,0:T(8,128)} %flow_x.1, s32[32,128]{1,0:T(8,128)} %param.9, s32[32,128]{1,0:T(8,128)} %param.8, f32[32,128]{1,0:T(8,128)} %flow_y.1), kind=kLoop, calls=%fused_computation.2 | loop fusion | flops 28672 | bytes 114688 | tf_op jit(solution)/shard_map/stack | solution.py:422
  1.4 0.0 copy-done.2
  1.5 3.1 %collective-permute-start.3 = (f32[4,32,128]{2,1,0:T(8,128)S(1)}, f32[4,32,128]{2,1,0:T(8,128)S(1)}, u32[]{:S(2)}, u32[]{:S(2)}) collective-permute-start(f32[4,32,128]{2,1,0:T(8,128)S(1)} %pad_maximum_fusion.own), channel_id=1, source_target_pairs={{0,8},{4,12},{8,4},{12,16},{16,24},{20,28},{24,20},{28,0},{1,9},{5... | collective-permute-start | bytes 196616 | tf_op jit(solution)/shard_map/ppermute | solution.py:54
  4.5 3.0 %collective-permute-start.2 = (f32[4,32,128]{2,1,0:T(8,128)S(1)}, f32[4,32,128]{2,1,0:T(8,128)S(1)}, u32[]{:S(2)}, u32[]{:S(2)}) collective-permute-start(f32[4,32,128]{2,1,0:T(8,128)S(1)} %pad_maximum_fusion.own), channel_id=1, source_target_pairs={{0,28},{4,8},{8,16},{12,20},{16,12},{20,24},{24,0},{28,4},{1,29},{... | collective-permute-start | bytes 196616 | tf_op jit(solution)/shard_map/ppermute | solution.py:54
  7.5 0.0 collective-permute-start.1
  7.6 2.3 %collective-permute-start = (f32[4,16,128]{2,1,0:T(8,128)S(1)}, f32[4,16,128]{2,1,0:T(8,128)S(1)}, u32[]{:S(2)}, u32[]{:S(2)}) collective-permute-start(f32[4,16,128]{2,1,0:T(8,128)S(1)} %slice.4), channel_id=1, source_target_pairs={{0,24},{4,28},{8,0},{12,4},{16,8},{20,12},{24,16},{28,20},{1,25},{... | collective-permute-start | bytes 98312 | tf_op jit(solution)/shard_map/ppermute | solution.py:54
  9.8 1.7 %collective-permute-done.got_4 = f32[4,16,128]{2,1,0:T(8,128)S(1)} collective-permute-done((f32[4,16,128]{2,1,0:T(8,128)S(1)}, f32[4,16,128]{2,1,0:T(8,128)S(1)}, u32[]{:S(2)}, u32[]{:S(2)}) %collective-permute-start) | collective-permute-done | bytes 32800 | tf_op jit(solution)/shard_map/ppermute | solution.py:54
  11.6 0.0 collective-permute-done.3.got_1
  11.6 0.0 collective-permute-done.2.got_2
  11.6 0.2 collective-permute-done.1.got_3
  11.8 0.0 copy-start
  11.8 0.0 copy-start.1
  11.8 0.2 %turn.1 = (f32[3,128,128]{2,1,0:T(8,128)S(1)}, f32[128,128]{1,0:T(8,128)S(1)}, f32[128,128]{1,0:T(8,128)S(1)}, f32[16,128]{1,0:T(8,128)S(1)}) custom-call(f32[4,16,128]{2,1,0:T(8,128)S(1)} %collective-permute-done.got_4, f32[4,32,128]{2,1,0:T(8,128)S(1)} %collective-permute-done.1.got_3, f32[4,32,128]{2,1,0:T(8,128)S(1)} %collective-permute-done.2.got_2, ...), custom_call_target="tpu_custom_call" | custom-call | tf_op jit(solution)/shard_map/turn/pallas_call | solution.py:429
  12.1 0.2 %collective-permute-start.4 = (f32[128,128]{1,0:T(8,128)S(1)}, f32[128,128]{1,0:T(8,128)S(1)}, u32[]{:S(2)}, u32[]{:S(2)}) collective-permute-start(f32[128,128]{1,0:T(8,128)S(1)} %get-tuple-element.7), channel_id=1, source_target_pairs={{0,3},{1,2},{2,1},{3,0},{4,7},{5,6},{6,5},{7,4},{8,11},{9,10},{10,... | collective-permute-start | bytes 196616 | tf_op jit(solution)/shard_map/ppermute | solution.py:54
  12.3 1.6 %collective-permute-start.5 = (f32[128,128]{1,0:T(8,128)S(1)}, f32[128,128]{1,0:T(8,128)S(1)}, u32[]{:S(2)}, u32[]{:S(2)}) collective-permute-start(f32[128,128]{1,0:T(8,128)S(1)} %get-tuple-element.8), channel_id=1, source_target_pairs={{0,1},{1,0},{2,3},{3,2},{4,5},{5,4},{6,7},{7,6},{8,9},{9,8},{10,11... | collective-permute-start | bytes 196616 | tf_op jit(solution)/shard_map/ppermute | solution.py:54
  13.9 2.4 %collective-permute-done.4.outer = f32[128,128]{1,0:T(8,128)S(1)} collective-permute-done((f32[128,128]{1,0:T(8,128)S(1)}, f32[128,128]{1,0:T(8,128)S(1)}, u32[]{:S(2)}, u32[]{:S(2)}) %collective-permute-start.4) | collective-permute-done | bytes 65568 | tf_op jit(solution)/shard_map/ppermute | solution.py:54
  16.3 0.0 collective-permute-done.5.inner
  16.3 0.0 copy-done
  16.3 0.0 copy-done.1
  16.3 6.5 %steps.1 = (f32[32,128]{1,0:T(8,128)}, f32[32,128]{1,0:T(8,128)}, f32[32,128]{1,0:T(8,128)}) custom-call(f32[128,128]{1,0:T(8,128)S(1)} %collective-permute-done.4.outer, f32[128,128]{1,0:T(8,128)S(1)} %collective-permute-done.5.inner, f32[3,128,128]{2,1,0:T(8,128)S(1)} %get-tuple-element.9.centre, f32[16,128]{1,0:T(8,128)S(1)} %get-tuple-element.10.ends, ...), custom_call_target="tpu_custom_call" | custom-call | tf_op jit(solution)/shard_map/steps/pallas_call | solution.py:445
  (2 shorter events, 0.0 us)
Async XLA Ops:
  0.6 0.8 %copy-start.2 = (f32[32,128]{1,0:T(8,128)S(1)}, f32[32,128]{1,0:T(8,128)}, u32[]{:S(2)}) copy-start(f32[32,128]{1,0:T(8,128)} %param.5) | copy-start | bytes 49156
  1.5 10.1 %collective-permute-start.3 = (f32[4,32,128]{2,1,0:T(8,128)S(1)}, f32[4,32,128]{2,1,0:T(8,128)S(1)}, u32[]{:S(2)}, u32[]{:S(2)}) collective-permute-start(f32[4,32,128]{2,1,0:T(8,128)S(1)} %pad_maximum_fusion.own), channel_id=1, source_target_pairs={{0,8},{4,12},{8,4},{12,16},{16,24},{20,28},{24,20},{28,0},{1,9},{5... | collective-permute-start | bytes 196616 | tf_op jit(solution)/shard_map/ppermute | solution.py:54
  4.5 7.1 %collective-permute-start.2 = (f32[4,32,128]{2,1,0:T(8,128)S(1)}, f32[4,32,128]{2,1,0:T(8,128)S(1)}, u32[]{:S(2)}, u32[]{:S(2)}) collective-permute-start(f32[4,32,128]{2,1,0:T(8,128)S(1)} %pad_maximum_fusion.own), channel_id=1, source_target_pairs={{0,28},{4,8},{8,16},{12,20},{16,12},{20,24},{24,0},{28,4},{1,29},{... | collective-permute-start | bytes 196616 | tf_op jit(solution)/shard_map/ppermute | solution.py:54
  7.5 4.3 %collective-permute-start.1 = (f32[4,32,128]{2,1,0:T(8,128)S(1)}, f32[4,32,128]{2,1,0:T(8,128)S(1)}, u32[]{:S(2)}, u32[]{:S(2)}) collective-permute-start(f32[4,32,128]{2,1,0:T(8,128)S(1)} %pad_maximum_fusion.own), channel_id=1, source_target_pairs={{0,4},{4,0},{8,12},{12,8},{16,20},{20,16},{24,28},{28,24},{1,5},{5... | collective-permute-start | bytes 196616 | tf_op jit(solution)/shard_map/ppermute | solution.py:54
  7.6 4.0 %collective-permute-start = (f32[4,16,128]{2,1,0:T(8,128)S(1)}, f32[4,16,128]{2,1,0:T(8,128)S(1)}, u32[]{:S(2)}, u32[]{:S(2)}) collective-permute-start(f32[4,16,128]{2,1,0:T(8,128)S(1)} %slice.4), channel_id=1, source_target_pairs={{0,24},{4,28},{8,0},{12,4},{16,8},{20,12},{24,16},{28,20},{1,25},{... | collective-permute-start | bytes 98312 | tf_op jit(solution)/shard_map/ppermute | solution.py:54
  11.8 4.5 %copy-start = (f32[32,128]{1,0:T(8,128)S(1)}, f32[32,128]{1,0:T(8,128)}, u32[]{:S(2)}) copy-start(f32[32,128]{1,0:T(8,128)} %flow_x.1) | copy-start | bytes 49156
  11.8 4.5 %copy-start.1 = (f32[32,128]{1,0:T(8,128)S(1)}, f32[32,128]{1,0:T(8,128)}, u32[]{:S(2)}) copy-start(f32[32,128]{1,0:T(8,128)} %flow_y.1) | copy-start | bytes 49156
  12.1 4.2 %collective-permute-start.4 = (f32[128,128]{1,0:T(8,128)S(1)}, f32[128,128]{1,0:T(8,128)S(1)}, u32[]{:S(2)}, u32[]{:S(2)}) collective-permute-start(f32[128,128]{1,0:T(8,128)S(1)} %get-tuple-element.7), channel_id=1, source_target_pairs={{0,3},{1,2},{2,1},{3,0},{4,7},{5,6},{6,5},{7,4},{8,11},{9,10},{10,... | collective-permute-start | bytes 196616 | tf_op jit(solution)/shard_map/ppermute | solution.py:54
  12.3 4.0 %collective-permute-start.5 = (f32[128,128]{1,0:T(8,128)S(1)}, f32[128,128]{1,0:T(8,128)S(1)}, u32[]{:S(2)}, u32[]{:S(2)}) collective-permute-start(f32[128,128]{1,0:T(8,128)S(1)} %get-tuple-element.8), channel_id=1, source_target_pairs={{0,1},{1,0},{2,3},{3,2},{4,5},{5,4},{6,7},{7,6},{8,9},{9,8},{10,11... | collective-permute-start | bytes 196616 | tf_op jit(solution)/shard_map/ppermute | solution.py:54

commit v4 on v3

--- a/solution.py
+++ b/solution.py
@@ -19,7 +19,6 @@
 FULL = 32
 MOVE = 6
 LAST = 2
-UNROLL = 3
 VMEM_LIMIT = 8 * 1024 * 1024
 
 R = FRICTION
@@ -338,10 +337,13 @@
     for k in range(blocks):
         e[k] = rows[0, strided(k), :]
         g[k] = rows[1, strided(k), :]
-        total_e[k] = jnp.zeros((ROW, e.shape[2]), jnp.float32)
         set_coefficients(k, rows[2, strided(k), :])
 
-    def one_step(kind, count):
+    def weigh_in(k, parts, is_first):
+        now = parts[0] + weighted(W_MIX[1:4], parts[1:4])
+        total_e[k] = now if is_first else DAMP * total_e[k] + now
+
+    def one_step(kind, count, is_first=False):
         first, second = (
             tuple(kind(count, ref, *coefficients[4 * n:4 * n + 4]) for ref in refs)
             for n, refs in enumerate(((e, g), (e1, g1)))
@@ -352,17 +354,13 @@
 
         def finish_step(k):
             parts = (e[k], g[k], e1[k], g1[k], second[0].divergence(k), second[1].divergence(k))
-            total_e[k] = DAMP * total_e[k] + parts[0] + weighted(W_MIX[1:4], parts[1:4])
+            weigh_in(k, parts, is_first)
             e[k] = (parts[0] + parts[1]) + (parts[2] + parts[4]) + E_MIX * parts[3]
             g[k] = weighted(G_MIX, parts)
 
         return [(first, finish), (second, finish_step)]
 
-    def some_steps(_, carry):
-        emit(blocks, [sweep for _ in range(UNROLL) for sweep in one_step(Slope, blocks)])
-        return carry
-
-    lax.fori_loop(0, (STEPS - LAST) // UNROLL, some_steps, 0)
+    emit(blocks, [sweep for n in range(STEPS - LAST) for sweep in one_step(Slope, blocks, n == 0)])
 
     margin, half = MOVE * LAST, length // 2
     few = (half + 2 * margin) // ROW
@@ -380,25 +378,26 @@
         e[k], g[k], total_e[k], kept[k] = (folded(f, k) for f in (0, 1, 3, 2))
         set_coefficients(k, kept[k])
 
-    def last_step(_, carry):
-        emit(few, one_step(QuickSlope, few))
-        return carry
-
-    lax.fori_loop(0, LAST, last_step, 0)
-
     square = Memo(lambda k: kept[k] * kept[k] * (GRAVITY / 3.0 * W_SCALE))
     a = Memo(lambda k: -0.5 * GRAVITY * W_SCALE + 2.0 * square[k])
     b = Memo(lambda k: -0.5 * square[k])
     a_east, b_east = Memo(lambda k: turned(a[k], -1, 1)), Memo(lambda k: turned(b[k], -1, 1))
+    first = tuple(QuickSlope(few, ref, *coefficients[:4]) for ref in (e, g))
+    second = QuickSlope(few, e1, *coefficients[4:])
     slope = QuickSlope(few, total_e, a, b, a_east, b_east, diverge=False)
 
-    def finish_velocity(k):
+    def finish_first(k):
+        e1[k], g1[k] = first[0].divergence(k), first[1].divergence(k)
+        weigh_in(k, (e[k], g[k], e1[k], g1[k]), False)
+
+    def finish_last(k):
         at = pl.ds(k, ROW, stride=few)
-        rows[0, at, :] = e[k]
+        rows[0, at, :] = (e[k] + g[k]) + (e1[k] + second.divergence(k)) + E_MIX * g1[k]
         rows[1, at, :] = slope.x_west[k]
         rows[2, at, :] = slope.y[k]
 
-    emit(few, [((slope,), finish_velocity)])
+    before_last = [sweep for _ in range(LAST - 1) for sweep in one_step(QuickSlope, few)]
+    emit(few, before_last + [(first, finish_first), ((second, slope), finish_last)])
 
     def tile(f):
         width = out_e.shape[0]

time: 23.1 us -> 22.8 us (0.987)
  Pallas kernels: 6.78 us -> 6.49 us
    pallas_call x1, Pallas kernels: 6.53 us -> 6.25 us  [on_device(): pl.pallas_call(step_kernel, out_shape=tuple((jax.ShapeDtypeStruct((width,...]
where the time goes in v4:
time: 22.8 us; the launch traced here: 22.6 us
  starting transfers between devices  10.2 us (45%)
  Pallas kernels  6.49 us (28%)
  waiting for transfers between devices  4.39 us (19%)
  other arithmetic  0.79 us (3%)
  between operations  0.67 us (3%)
    ppermute x6, starting transfers between devices, move(): lax.ppermute(cells, axis, [(i, (i + steps[i % len(steps)]) % count) for i...  10.2 us
    pallas_call x1, Pallas kernels, on_device(): pl.pallas_call(step_kernel, out_shape=tuple((jax.ShapeDtypeStruct((width,...  6.25 us
    ppermute x6, waiting for transfers between devices, move(): lax.ppermute(cells, axis, [(i, (i + steps[i % len(steps)]) % count) for i...  4.39 us
    another operation x2, other arithmetic, on_device(): own = jnp.stack([surface, depth * velocity_x, depth * velocity_y, depth])  0.79 us
  transfers between devices with their start and end apart: 6, of which 3 were waited for; matrix products, arithmetic and copies ran while one was open for 0% of the time, Pallas kernels for 0%

profile of v4, /device:TPU:0, one launch (start us, length us, event | category | flops | bytes accessed | tf_op | source)
XLA Modules:
  0.0 22.6 jit_solution(2403234432234299546)
XLA Ops:
  0.6 0.0 copy-start.2
  0.6 0.8 %multiply_bitcast_fusion.1 = (f32[1,32,128]{2,1,0:T(8,128)S(1)}, f32[1,32,128]{2,1,0:T(8,128)S(1)}, f32[1,32,128]{2,1,0:T(8,128)S(1)}) fusion(f32[32,128]{1,0:T(8,128)} %flow_x.1, s32[32,128]{1,0:T(8,128)} %param.9, s32[32,128]{1,0:T(8,128)} %param.8, f32[32,128]{1,0:T(8,128)} %flow_y.1), kind=kLoop, calls=%fused_computation.2 | loop fusion | flops 28672 | bytes 114688 | tf_op jit(solution)/shard_map/stack | solution.py:421
  1.4 0.0 copy-done.2
  1.5 3.1 %collective-permute-start.3 = (f32[4,32,128]{2,1,0:T(8,128)S(1)}, f32[4,32,128]{2,1,0:T(8,128)S(1)}, u32[]{:S(2)}, u32[]{:S(2)}) collective-permute-start(f32[4,32,128]{2,1,0:T(8,128)S(1)} %pad_maximum_fusion.own), channel_id=1, source_target_pairs={{0,8},{4,12},{8,4},{12,16},{16,24},{20,28},{24,20},{28,0},{1,9},{5... | collective-permute-start | bytes 196616 | tf_op jit(solution)/shard_map/ppermute | solution.py:53
  4.5 3.0 %collective-permute-start.2 = (f32[4,32,128]{2,1,0:T(8,128)S(1)}, f32[4,32,128]{2,1,0:T(8,128)S(1)}, u32[]{:S(2)}, u32[]{:S(2)}) collective-permute-start(f32[4,32,128]{2,1,0:T(8,128)S(1)} %pad_maximum_fusion.own), channel_id=1, source_target_pairs={{0,28},{4,8},{8,16},{12,20},{16,12},{20,24},{24,0},{28,4},{1,29},{... | collective-permute-start | bytes 196616 | tf_op jit(solution)/shard_map/ppermute | solution.py:53
  7.5 0.0 collective-permute-start.1
  7.6 2.3 %collective-permute-start = (f32[4,16,128]{2,1,0:T(8,128)S(1)}, f32[4,16,128]{2,1,0:T(8,128)S(1)}, u32[]{:S(2)}, u32[]{:S(2)}) collective-permute-start(f32[4,16,128]{2,1,0:T(8,128)S(1)} %slice.4), channel_id=1, source_target_pairs={{0,24},{4,28},{8,0},{12,4},{16,8},{20,12},{24,16},{28,20},{1,25},{... | collective-permute-start | bytes 98312 | tf_op jit(solution)/shard_map/ppermute | solution.py:53
  9.8 1.7 %collective-permute-done.got_4 = f32[4,16,128]{2,1,0:T(8,128)S(1)} collective-permute-done((f32[4,16,128]{2,1,0:T(8,128)S(1)}, f32[4,16,128]{2,1,0:T(8,128)S(1)}, u32[]{:S(2)}, u32[]{:S(2)}) %collective-permute-start) | collective-permute-done | bytes 32800 | tf_op jit(solution)/shard_map/ppermute | solution.py:53
  11.6 0.0 collective-permute-done.3.got_1
  11.6 0.0 collective-permute-done.2.got_2
  11.6 0.2 collective-permute-done.1.got_3
  11.8 0.0 copy-start
  11.8 0.0 copy-start.1
  11.8 0.2 %turn.1 = (f32[3,128,128]{2,1,0:T(8,128)S(1)}, f32[128,128]{1,0:T(8,128)S(1)}, f32[128,128]{1,0:T(8,128)S(1)}, f32[16,128]{1,0:T(8,128)S(1)}) custom-call(f32[4,16,128]{2,1,0:T(8,128)S(1)} %collective-permute-done.got_4, f32[4,32,128]{2,1,0:T(8,128)S(1)} %collective-permute-done.1.got_3, f32[4,32,128]{2,1,0:T(8,128)S(1)} %collective-permute-done.2.got_2, ...), custom_call_target="tpu_custom_call" | custom-call | tf_op jit(solution)/shard_map/turn/pallas_call | solution.py:428
  12.1 0.2 %collective-permute-start.4 = (f32[128,128]{1,0:T(8,128)S(1)}, f32[128,128]{1,0:T(8,128)S(1)}, u32[]{:S(2)}, u32[]{:S(2)}) collective-permute-start(f32[128,128]{1,0:T(8,128)S(1)} %get-tuple-element.7), channel_id=1, source_target_pairs={{0,3},{1,2},{2,1},{3,0},{4,7},{5,6},{6,5},{7,4},{8,11},{9,10},{10,... | collective-permute-start | bytes 196616 | tf_op jit(solution)/shard_map/ppermute | solution.py:53
  12.3 1.6 %collective-permute-start.5 = (f32[128,128]{1,0:T(8,128)S(1)}, f32[128,128]{1,0:T(8,128)S(1)}, u32[]{:S(2)}, u32[]{:S(2)}) collective-permute-start(f32[128,128]{1,0:T(8,128)S(1)} %get-tuple-element.8), channel_id=1, source_target_pairs={{0,1},{1,0},{2,3},{3,2},{4,5},{5,4},{6,7},{7,6},{8,9},{9,8},{10,11... | collective-permute-start | bytes 196616 | tf_op jit(solution)/shard_map/ppermute | solution.py:53
  13.9 2.4 %collective-permute-done.4.outer = f32[128,128]{1,0:T(8,128)S(1)} collective-permute-done((f32[128,128]{1,0:T(8,128)S(1)}, f32[128,128]{1,0:T(8,128)S(1)}, u32[]{:S(2)}, u32[]{:S(2)}) %collective-permute-start.4) | collective-permute-done | bytes 65568 | tf_op jit(solution)/shard_map/ppermute | solution.py:53
  16.3 0.0 collective-permute-done.5.inner
  16.3 0.0 copy-done
  16.3 0.0 copy-done.1
  16.3 6.3 %steps.1 = (f32[32,128]{1,0:T(8,128)}, f32[32,128]{1,0:T(8,128)}, f32[32,128]{1,0:T(8,128)}) custom-call(f32[128,128]{1,0:T(8,128)S(1)} %collective-permute-done.4.outer, f32[128,128]{1,0:T(8,128)S(1)} %collective-permute-done.5.inner, f32[3,128,128]{2,1,0:T(8,128)S(1)} %get-tuple-element.9.centre, f32[16,128]{1,0:T(8,128)S(1)} %get-tuple-element.10.ends, ...), custom_call_target="tpu_custom_call" | custom-call | tf_op jit(solution)/shard_map/steps/pallas_call | solution.py:444
  (2 shorter events, 0.0 us)
Async XLA Ops:
  0.6 0.8 %copy-start.2 = (f32[32,128]{1,0:T(8,128)S(1)}, f32[32,128]{1,0:T(8,128)}, u32[]{:S(2)}) copy-start(f32[32,128]{1,0:T(8,128)} %param.5) | copy-start | bytes 49156
  1.5 10.1 %collective-permute-start.3 = (f32[4,32,128]{2,1,0:T(8,128)S(1)}, f32[4,32,128]{2,1,0:T(8,128)S(1)}, u32[]{:S(2)}, u32[]{:S(2)}) collective-permute-start(f32[4,32,128]{2,1,0:T(8,128)S(1)} %pad_maximum_fusion.own), channel_id=1, source_target_pairs={{0,8},{4,12},{8,4},{12,16},{16,24},{20,28},{24,20},{28,0},{1,9},{5... | collective-permute-start | bytes 196616 | tf_op jit(solution)/shard_map/ppermute | solution.py:53
  4.5 7.1 %collective-permute-start.2 = (f32[4,32,128]{2,1,0:T(8,128)S(1)}, f32[4,32,128]{2,1,0:T(8,128)S(1)}, u32[]{:S(2)}, u32[]{:S(2)}) collective-permute-start(f32[4,32,128]{2,1,0:T(8,128)S(1)} %pad_maximum_fusion.own), channel_id=1, source_target_pairs={{0,28},{4,8},{8,16},{12,20},{16,12},{20,24},{24,0},{28,4},{1,29},{... | collective-permute-start | bytes 196616 | tf_op jit(solution)/shard_map/ppermute | solution.py:53
  7.5 4.3 %collective-permute-start.1 = (f32[4,32,128]{2,1,0:T(8,128)S(1)}, f32[4,32,128]{2,1,0:T(8,128)S(1)}, u32[]{:S(2)}, u32[]{:S(2)}) collective-permute-start(f32[4,32,128]{2,1,0:T(8,128)S(1)} %pad_maximum_fusion.own), channel_id=1, source_target_pairs={{0,4},{4,0},{8,12},{12,8},{16,20},{20,16},{24,28},{28,24},{1,5},{5... | collective-permute-start | bytes 196616 | tf_op jit(solution)/shard_map/ppermute | solution.py:53
  7.6 4.0 %collective-permute-start = (f32[4,16,128]{2,1,0:T(8,128)S(1)}, f32[4,16,128]{2,1,0:T(8,128)S(1)}, u32[]{:S(2)}, u32[]{:S(2)}) collective-permute-start(f32[4,16,128]{2,1,0:T(8,128)S(1)} %slice.4), channel_id=1, source_target_pairs={{0,24},{4,28},{8,0},{12,4},{16,8},{20,12},{24,16},{28,20},{1,25},{... | collective-permute-start | bytes 98312 | tf_op jit(solution)/shard_map/ppermute | solution.py:53
  11.8 4.5 %copy-start = (f32[32,128]{1,0:T(8,128)S(1)}, f32[32,128]{1,0:T(8,128)}, u32[]{:S(2)}) copy-start(f32[32,128]{1,0:T(8,128)} %flow_x.1) | copy-start | bytes 49156
  11.8 4.5 %copy-start.1 = (f32[32,128]{1,0:T(8,128)S(1)}, f32[32,128]{1,0:T(8,128)}, u32[]{:S(2)}) copy-start(f32[32,128]{1,0:T(8,128)} %flow_y.1) | copy-start | bytes 49156
  12.1 4.2 %collective-permute-start.4 = (f32[128,128]{1,0:T(8,128)S(1)}, f32[128,128]{1,0:T(8,128)S(1)}, u32[]{:S(2)}, u32[]{:S(2)}) collective-permute-start(f32[128,128]{1,0:T(8,128)S(1)} %get-tuple-element.7), channel_id=1, source_target_pairs={{0,3},{1,2},{2,1},{3,0},{4,7},{5,6},{6,5},{7,4},{8,11},{9,10},{10,... | collective-permute-start | bytes 196616 | tf_op jit(solution)/shard_map/ppermute | solution.py:53
  12.3 4.0 %collective-permute-start.5 = (f32[128,128]{1,0:T(8,128)S(1)}, f32[128,128]{1,0:T(8,128)S(1)}, u32[]{:S(2)}, u32[]{:S(2)}) collective-permute-start(f32[128,128]{1,0:T(8,128)S(1)} %get-tuple-element.8), channel_id=1, source_target_pairs={{0,1},{1,0},{2,3},{3,2},{4,5},{5,4},{6,7},{7,6},{8,9},{9,8},{10,11... | collective-permute-start | bytes 196616 | tf_op jit(solution)/shard_map/ppermute | solution.py:53

commit v5 on v4

--- a/solution.py
+++ b/solution.py
@@ -40,10 +40,11 @@
 DAMP = sum(TAYLOR[n] * (-R) ** n for n in range(5))
 
 G_SCALE = E_NEXT[1]
-K_SCALE = (E_NEXT[2], E_NEXT[4] / E_NEXT[2])
+K_SCALE = E_NEXT[2]
 W_SCALE = W_NEXT[0]
-KEPT = (1.0, G_SCALE, K_SCALE[0], G_SCALE * K_SCALE[0], K_SCALE[0] * K_SCALE[1], G_SCALE * K_SCALE[0] * K_SCALE[1])
+KEPT = (1.0, G_SCALE, K_SCALE, G_SCALE * K_SCALE, K_SCALE**2, G_SCALE * K_SCALE**2)
 E_MIX = E_NEXT[3] / KEPT[3]
+E_MIX_2 = E_NEXT[4] / KEPT[4]
 G_MIX = [G_SCALE * weight / kept for weight, kept in zip(G_NEXT, KEPT)]
 W_MIX = [weight / (W_SCALE * kept) for weight, kept in zip(W_NEXT, KEPT)]
 
@@ -146,7 +147,7 @@
 
 
 class Slope:
-    AHEAD, LAG, SEAM = 5, 8, 2
+    AHEAD, LAG, SEAM = 6, 7, 1
     EDGE = ("slope_y",)
 
     @classmethod
@@ -327,12 +328,11 @@
         return pl.ds(k, ROW, stride=blocks)
 
     def set_coefficients(k, depth):
-        cube = depth * depth * depth * (GRAVITY / 12.0)
-        slow = 0.25 * GRAVITY * depth - 4.0 * cube
-        both = (slow, cube, turned(slow, -1, 1), turned(cube, -1, 1))
-        for n in range(2):
-            for ref, value in zip(coefficients[4 * n:4 * n + 4], both):
-                ref[k] = K_SCALE[n] * value
+        cube = depth * depth * depth * (GRAVITY / 12.0 * K_SCALE)
+        slow = 0.25 * GRAVITY * K_SCALE * depth - 4.0 * cube
+        values = (slow, cube, turned(slow, -1, 1), turned(cube, -1, 1))
+        for ref, value in zip(coefficients, values):
+            ref[k] = value
 
     for k in range(blocks):
         e[k] = rows[0, strided(k), :]
@@ -345,8 +345,7 @@
 
     def one_step(kind, count, is_first=False):
         first, second = (
-            tuple(kind(count, ref, *coefficients[4 * n:4 * n + 4]) for ref in refs)
-            for n, refs in enumerate(((e, g), (e1, g1)))
+            tuple(kind(count, ref, *coefficients) for ref in refs) for refs in ((e, g), (e1, g1))
         )
 
         def finish(k):
@@ -355,7 +354,7 @@
         def finish_step(k):
             parts = (e[k], g[k], e1[k], g1[k], second[0].divergence(k), second[1].divergence(k))
             weigh_in(k, parts, is_first)
-            e[k] = (parts[0] + parts[1]) + (parts[2] + parts[4]) + E_MIX * parts[3]
+            e[k] = (parts[0] + parts[1]) + (parts[2] + E_MIX * parts[3]) + E_MIX_2 * parts[4]
             g[k] = weighted(G_MIX, parts)
 
         return [(first, finish), (second, finish_step)]
@@ -382,8 +381,8 @@
     a = Memo(lambda k: -0.5 * GRAVITY * W_SCALE + 2.0 * square[k])
     b = Memo(lambda k: -0.5 * square[k])
     a_east, b_east = Memo(lambda k: turned(a[k], -1, 1)), Memo(lambda k: turned(b[k], -1, 1))
-    first = tuple(QuickSlope(few, ref, *coefficients[:4]) for ref in (e, g))
-    second = QuickSlope(few, e1, *coefficients[4:])
+    first = tuple(QuickSlope(few, ref, *coefficients) for ref in (e, g))
+    second = QuickSlope(few, e1, *coefficients)
     slope = QuickSlope(few, total_e, a, b, a_east, b_east, diverge=False)
 
     def finish_first(k):
@@ -392,7 +391,7 @@
 
     def finish_last(k):
         at = pl.ds(k, ROW, stride=few)
-        rows[0, at, :] = (e[k] + g[k]) + (e1[k] + second.divergence(k)) + E_MIX * g1[k]
+        rows[0, at, :] = (e[k] + g[k]) + (e1[k] + E_MIX * g1[k]) + E_MIX_2 * second.divergence(k)
         rows[1, at, :] = slope.x_west[k]
         rows[2, at, :] = slope.y[k]
 
@@ -444,7 +443,7 @@
     return pl.pallas_call(
         step_kernel,
         out_shape=tuple(jax.ShapeDtypeStruct((width, length), f32) for _ in range(3)),
-        scratch_shapes=[pltpu.VMEM((4, total, lanes), f32)] + [pltpu.VMEM(packet.shape, f32)] * 2 + [blocked] * 14,
+        scratch_shapes=[pltpu.VMEM((4, total, lanes), f32)] + [pltpu.VMEM(packet.shape, f32)] * 2 + [blocked] * 10,
         compiler_params=pltpu.CompilerParams(vmem_limit_bytes=VMEM_LIMIT),
         name="steps",
     )(outer, inner, centre, ends, own, velocity_x, velocity_y)

time: 22.8 us -> 22.7 us (level)
  no operation moved by 1% of the time
where the time goes in v5:
time: 22.7 us; the launch traced here: 22.4 us
  starting transfers between devices  10.2 us (45%)
  Pallas kernels  6.35 us (28%)
  waiting for transfers between devices  4.39 us (19%)
  other arithmetic  0.79 us (3%)
  between operations  0.67 us (3%)
    ppermute x6, starting transfers between devices, move(): lax.ppermute(cells, axis, [(i, (i + steps[i % len(steps)]) % count) for i...  10.2 us
    pallas_call x1, Pallas kernels, on_device(): pl.pallas_call(step_kernel, out_shape=tuple((jax.ShapeDtypeStruct((width,...  6.11 us
    ppermute x6, waiting for transfers between devices, move(): lax.ppermute(cells, axis, [(i, (i + steps[i % len(steps)]) % count) for i...  4.39 us
    another operation x2, other arithmetic, on_device(): own = jnp.stack([surface, depth * velocity_x, depth * velocity_y, depth])  0.79 us
  transfers between devices with their start and end apart: 6, of which 3 were waited for; matrix products, arithmetic and copies ran while one was open for 0% of the time, Pallas kernels for 0%

profile of v5, /device:TPU:0, one launch (start us, length us, event | category | flops | bytes accessed | tf_op | source)
XLA Modules:
  0.0 22.4 jit_solution(5200101572496209135)
XLA Ops:
  0.6 0.0 copy-start.2
  0.6 0.8 %multiply_bitcast_fusion.1 = (f32[1,32,128]{2,1,0:T(8,128)S(1)}, f32[1,32,128]{2,1,0:T(8,128)S(1)}, f32[1,32,128]{2,1,0:T(8,128)S(1)}) fusion(f32[32,128]{1,0:T(8,128)} %flow_x.1, s32[32,128]{1,0:T(8,128)} %param.9, s32[32,128]{1,0:T(8,128)} %param.8, f32[32,128]{1,0:T(8,128)} %flow_y.1), kind=kLoop, calls=%fused_computation.2 | loop fusion | flops 28672 | bytes 114688 | tf_op jit(solution)/shard_map/stack | solution.py:420
  1.4 0.0 copy-done.2
  1.5 3.1 %collective-permute-start.3 = (f32[4,32,128]{2,1,0:T(8,128)S(1)}, f32[4,32,128]{2,1,0:T(8,128)S(1)}, u32[]{:S(2)}, u32[]{:S(2)}) collective-permute-start(f32[4,32,128]{2,1,0:T(8,128)S(1)} %pad_maximum_fusion.own), channel_id=1, source_target_pairs={{0,8},{4,12},{8,4},{12,16},{16,24},{20,28},{24,20},{28,0},{1,9},{5... | collective-permute-start | bytes 196616 | tf_op jit(solution)/shard_map/ppermute | solution.py:54
  4.5 3.0 %collective-permute-start.2 = (f32[4,32,128]{2,1,0:T(8,128)S(1)}, f32[4,32,128]{2,1,0:T(8,128)S(1)}, u32[]{:S(2)}, u32[]{:S(2)}) collective-permute-start(f32[4,32,128]{2,1,0:T(8,128)S(1)} %pad_maximum_fusion.own), channel_id=1, source_target_pairs={{0,28},{4,8},{8,16},{12,20},{16,12},{20,24},{24,0},{28,4},{1,29},{... | collective-permute-start | bytes 196616 | tf_op jit(solution)/shard_map/ppermute | solution.py:54
  7.5 0.0 collective-permute-start.1
  7.6 2.3 %collective-permute-start = (f32[4,16,128]{2,1,0:T(8,128)S(1)}, f32[4,16,128]{2,1,0:T(8,128)S(1)}, u32[]{:S(2)}, u32[]{:S(2)}) collective-permute-start(f32[4,16,128]{2,1,0:T(8,128)S(1)} %slice.4), channel_id=1, source_target_pairs={{0,24},{4,28},{8,0},{12,4},{16,8},{20,12},{24,16},{28,20},{1,25},{... | collective-permute-start | bytes 98312 | tf_op jit(solution)/shard_map/ppermute | solution.py:54
  9.8 1.7 %collective-permute-done.got_4 = f32[4,16,128]{2,1,0:T(8,128)S(1)} collective-permute-done((f32[4,16,128]{2,1,0:T(8,128)S(1)}, f32[4,16,128]{2,1,0:T(8,128)S(1)}, u32[]{:S(2)}, u32[]{:S(2)}) %collective-permute-start) | collective-permute-done | bytes 32800 | tf_op jit(solution)/shard_map/ppermute | solution.py:54
  11.6 0.0 collective-permute-done.3.got_1
  11.6 0.0 collective-permute-done.2.got_2
  11.6 0.2 collective-permute-done.1.got_3
  11.8 0.0 copy-start
  11.8 0.0 copy-start.1
  11.8 0.2 %turn.1 = (f32[3,128,128]{2,1,0:T(8,128)S(1)}, f32[128,128]{1,0:T(8,128)S(1)}, f32[128,128]{1,0:T(8,128)S(1)}, f32[16,128]{1,0:T(8,128)S(1)}) custom-call(f32[4,16,128]{2,1,0:T(8,128)S(1)} %collective-permute-done.got_4, f32[4,32,128]{2,1,0:T(8,128)S(1)} %collective-permute-done.1.got_3, f32[4,32,128]{2,1,0:T(8,128)S(1)} %collective-permute-done.2.got_2, ...), custom_call_target="tpu_custom_call" | custom-call | tf_op jit(solution)/shard_map/turn/pallas_call | solution.py:427
  12.1 0.2 %collective-permute-start.4 = (f32[128,128]{1,0:T(8,128)S(1)}, f32[128,128]{1,0:T(8,128)S(1)}, u32[]{:S(2)}, u32[]{:S(2)}) collective-permute-start(f32[128,128]{1,0:T(8,128)S(1)} %get-tuple-element.7), channel_id=1, source_target_pairs={{0,3},{1,2},{2,1},{3,0},{4,7},{5,6},{6,5},{7,4},{8,11},{9,10},{10,... | collective-permute-start | bytes 196616 | tf_op jit(solution)/shard_map/ppermute | solution.py:54
  12.3 1.6 %collective-permute-start.5 = (f32[128,128]{1,0:T(8,128)S(1)}, f32[128,128]{1,0:T(8,128)S(1)}, u32[]{:S(2)}, u32[]{:S(2)}) collective-permute-start(f32[128,128]{1,0:T(8,128)S(1)} %get-tuple-element.8), channel_id=1, source_target_pairs={{0,1},{1,0},{2,3},{3,2},{4,5},{5,4},{6,7},{7,6},{8,9},{9,8},{10,11... | collective-permute-start | bytes 196616 | tf_op jit(solution)/shard_map/ppermute | solution.py:54
  13.9 2.4 %collective-permute-done.4.outer = f32[128,128]{1,0:T(8,128)S(1)} collective-permute-done((f32[128,128]{1,0:T(8,128)S(1)}, f32[128,128]{1,0:T(8,128)S(1)}, u32[]{:S(2)}, u32[]{:S(2)}) %collective-permute-start.4) | collective-permute-done | bytes 65568 | tf_op jit(solution)/shard_map/ppermute | solution.py:54
  16.3 0.0 collective-permute-done.5.inner
  16.3 0.0 copy-done
  16.3 0.0 copy-done.1
  16.3 6.1 %steps.1 = (f32[32,128]{1,0:T(8,128)}, f32[32,128]{1,0:T(8,128)}, f32[32,128]{1,0:T(8,128)}) custom-call(f32[128,128]{1,0:T(8,128)S(1)} %collective-permute-done.4.outer, f32[128,128]{1,0:T(8,128)S(1)} %collective-permute-done.5.inner, f32[3,128,128]{2,1,0:T(8,128)S(1)} %get-tuple-element.9.centre, f32[16,128]{1,0:T(8,128)S(1)} %get-tuple-element.10.ends, ...), custom_call_target="tpu_custom_call" | custom-call | tf_op jit(solution)/shard_map/steps/pallas_call | solution.py:443
  (2 shorter events, 0.0 us)
Async XLA Ops:
  0.6 0.8 %copy-start.2 = (f32[32,128]{1,0:T(8,128)S(1)}, f32[32,128]{1,0:T(8,128)}, u32[]{:S(2)}) copy-start(f32[32,128]{1,0:T(8,128)} %param.5) | copy-start | bytes 49156
  1.5 10.1 %collective-permute-start.3 = (f32[4,32,128]{2,1,0:T(8,128)S(1)}, f32[4,32,128]{2,1,0:T(8,128)S(1)}, u32[]{:S(2)}, u32[]{:S(2)}) collective-permute-start(f32[4,32,128]{2,1,0:T(8,128)S(1)} %pad_maximum_fusion.own), channel_id=1, source_target_pairs={{0,8},{4,12},{8,4},{12,16},{16,24},{20,28},{24,20},{28,0},{1,9},{5... | collective-permute-start | bytes 196616 | tf_op jit(solution)/shard_map/ppermute | solution.py:54
  4.5 7.1 %collective-permute-start.2 = (f32[4,32,128]{2,1,0:T(8,128)S(1)}, f32[4,32,128]{2,1,0:T(8,128)S(1)}, u32[]{:S(2)}, u32[]{:S(2)}) collective-permute-start(f32[4,32,128]{2,1,0:T(8,128)S(1)} %pad_maximum_fusion.own), channel_id=1, source_target_pairs={{0,28},{4,8},{8,16},{12,20},{16,12},{20,24},{24,0},{28,4},{1,29},{... | collective-permute-start | bytes 196616 | tf_op jit(solution)/shard_map/ppermute | solution.py:54
  7.5 4.3 %collective-permute-start.1 = (f32[4,32,128]{2,1,0:T(8,128)S(1)}, f32[4,32,128]{2,1,0:T(8,128)S(1)}, u32[]{:S(2)}, u32[]{:S(2)}) collective-permute-start(f32[4,32,128]{2,1,0:T(8,128)S(1)} %pad_maximum_fusion.own), channel_id=1, source_target_pairs={{0,4},{4,0},{8,12},{12,8},{16,20},{20,16},{24,28},{28,24},{1,5},{5... | collective-permute-start | bytes 196616 | tf_op jit(solution)/shard_map/ppermute | solution.py:54
  7.6 4.0 %collective-permute-start = (f32[4,16,128]{2,1,0:T(8,128)S(1)}, f32[4,16,128]{2,1,0:T(8,128)S(1)}, u32[]{:S(2)}, u32[]{:S(2)}) collective-permute-start(f32[4,16,128]{2,1,0:T(8,128)S(1)} %slice.4), channel_id=1, source_target_pairs={{0,24},{4,28},{8,0},{12,4},{16,8},{20,12},{24,16},{28,20},{1,25},{... | collective-permute-start | bytes 98312 | tf_op jit(solution)/shard_map/ppermute | solution.py:54
  11.8 4.5 %copy-start = (f32[32,128]{1,0:T(8,128)S(1)}, f32[32,128]{1,0:T(8,128)}, u32[]{:S(2)}) copy-start(f32[32,128]{1,0:T(8,128)} %flow_x.1) | copy-start | bytes 49156
  11.8 4.5 %copy-start.1 = (f32[32,128]{1,0:T(8,128)S(1)}, f32[32,128]{1,0:T(8,128)}, u32[]{:S(2)}) copy-start(f32[32,128]{1,0:T(8,128)} %flow_y.1) | copy-start | bytes 49156
  12.1 4.2 %collective-permute-start.4 = (f32[128,128]{1,0:T(8,128)S(1)}, f32[128,128]{1,0:T(8,128)S(1)}, u32[]{:S(2)}, u32[]{:S(2)}) collective-permute-start(f32[128,128]{1,0:T(8,128)S(1)} %get-tuple-element.7), channel_id=1, source_target_pairs={{0,3},{1,2},{2,1},{3,0},{4,7},{5,6},{6,5},{7,4},{8,11},{9,10},{10,... | collective-permute-start | bytes 196616 | tf_op jit(solution)/shard_map/ppermute | solution.py:54
  12.3 4.0 %collective-permute-start.5 = (f32[128,128]{1,0:T(8,128)S(1)}, f32[128,128]{1,0:T(8,128)S(1)}, u32[]{:S(2)}, u32[]{:S(2)}) collective-permute-start(f32[128,128]{1,0:T(8,128)S(1)} %get-tuple-element.8), channel_id=1, source_target_pairs={{0,1},{1,0},{2,3},{3,2},{4,5},{5,4},{6,7},{7,6},{8,9},{9,8},{10,11... | collective-permute-start | bytes 196616 | tf_op jit(solution)/shard_map/ppermute | solution.py:54
